TPU v7x, 32 devices: a whole 2x2x4 slice. The times are simulated.
32 devices in a mesh: tm: 8 (over z, core), space: 4 (over y, x).
Axes of the slice: x: 2, y: 2, z: 4, core: 2. Of those that a mesh axis runs over, the one named last changes fastest.
Arguments:
- sections: int32 [8], replicated, may hold values from 1 to 4, 20 in all
- right_side: bfloat16 [32, 64, 2048], P('tm'), may hold values from -6 to 6
- tip_side: float32 [64, 8], replicated, may hold values from -48 to 48
- diag_inverse: bfloat16 [32, 2048, 2048], P('tm', 'space'), may hold values from -0.08 to 0.42, as said below
- forward_coupling: bfloat16 [32, 2048, 128], P('tm', 'space'), may hold values from -1 to 1
- backward_coupling: bfloat16 [32, 2048, 128], P('tm', 'space'), may hold values from -1 to 1
- arrow_rows: bfloat16 [32, 8, 2048], P('tm', None, 'space'), may hold values from -3.3 to 3.3
- tip_inverse: float32 [8, 8], replicated, may hold values from -0.4 to 0.4, as said below
Outputs:
- solution: float32 [32, 64, 2048], P('tm', None, 'space')
- tip_solution: float32 [64, 8], replicated
Inputs may be any that keep to these rules, and one draw needn't show every extreme that they name: Section i holds the live slots i * 4 to i * 4 + sections[i] - 1. `diag_inverse`: each block is lower triangular with a positive diagonal. `tip_inverse`: lower triangular with a positive diagonal.
All inputs are finite; a program needn't handle non-finite values.
Results may differ from a plain program's by a relative error of at most 0.0031.
Values sent between devices are 32-bit elements; how exact they have to be, the bound alone decides.
A program may use at most 64 MiB of HBM per device.

v0:
```python
import jax
import jax.numpy as jnp
from jax import lax
from jax.sharding import PartitionSpec as P


def prefix(value, axis, join, neutral, backward):
    count, mine = (lax.axis_size(axis), lax.axis_index(axis))
    pieces = jax.tree.map(lambda part: lax.all_gather(part, axis), value)
    if backward:
        pieces = jax.tree.map(lambda part: part[::-1], pieces)
        mine = count - 1 - mine
    running = jax.tree.map(
        lambda part, zero: jnp.full_like(part, 0) + jnp.asarray(zero, part.dtype), value, neutral
    )

    def lap(position, running):
        longer = join(running, jax.tree.map(lambda part: part[position], pieces))
        return jax.tree.map(lambda new, old: jnp.where(position < mine, new, old), longer, running)

    return lax.fori_loop(0, count - 1, lap, running)


def shifted(value, axis, steps):
    count = lax.axis_size(axis)
    leading, last = (max(0, -steps), min(count, count - steps))
    return lax.ppermute(value, axis, [(source, source + steps) for source in range(leading, last)])


def couple(states, coupling):
    row_count, node_width = states.shape
    sub_width = coupling.shape[1]
    sub_count = node_width // sub_width
    shaped = states.reshape(row_count, sub_count, sub_width)
    blocks = coupling.astype(jnp.float32).reshape(sub_count, sub_width, sub_width)
    return jnp.einsum("rnk,nik->rni", shaped, blocks, precision=lax.Precision.HIGHEST).reshape(
        row_count, node_width
    )


def apply_map(offset, mapping):
    row_count, node_width = offset.shape
    sub_count, sub_width = (mapping.shape[0], mapping.shape[1])
    shaped = offset.reshape(row_count, sub_count, sub_width)
    return jnp.einsum("rni,nik->rnk", shaped, mapping, precision=lax.Precision.HIGHEST).reshape(
        row_count, node_width
    )


def compose(earlier, later):
    mapping = jnp.einsum("nij,njk->nik", earlier[0], later[0], precision=lax.Precision.HIGHEST)
    return (mapping, apply_map(earlier[1], later[0]) + later[1])


def section_map(driven, couplings, live_count, order):
    row_count, node_width = (driven.shape[1], driven.shape[2])
    sub_width = couplings.shape[2]
    sub_count = node_width // sub_width
    mapping = jnp.broadcast_to(
        jnp.eye(sub_width, dtype=jnp.float32), (sub_count, sub_width, sub_width)
    )
    offset = jnp.zeros((row_count, node_width), jnp.float32)
    for slot_index in order:
        blocks = couplings[slot_index].astype(jnp.float32).reshape(sub_count, sub_width, sub_width)
        new_offset = driven[slot_index] - couple(offset, couplings[slot_index])
        new_mapping = -jnp.einsum("nij,nkj->nik", mapping, blocks, precision=lax.Precision.HIGHEST)
        live_flag = slot_index < live_count
        offset = jnp.where(live_flag, new_offset, offset)
        mapping = jnp.where(live_flag, new_mapping, mapping)
    return (mapping, offset)


def resolve(incoming, driven, couplings, live_count, order):
    outputs = [None] * driven.shape[0]
    previous = incoming
    for slot_index in order:
        update = driven[slot_index] - couple(previous, couplings[slot_index])
        live_flag = slot_index < live_count
        outputs[slot_index] = jnp.where(live_flag, update, jnp.float32(0.0))
        previous = jnp.where(live_flag, update, previous)
    return jnp.stack(outputs, 0)


def on_device(
    sections,
    right_side,
    tip_side,
    diag_inverse,
    forward_coupling,
    backward_coupling,
    arrow_rows,
    tip_inverse,
):
    slot_count = diag_inverse.shape[0]
    position = lax.axis_index("tm")
    section_len = lax.dynamic_index_in_dim(sections, position, 0, keepdims=False)
    forward_order = list(range(slot_count))
    backward_order = list(reversed(range(slot_count)))
    driven = jnp.einsum(
        "trs,tqs->trq", right_side, diag_inverse, preferred_element_type=jnp.float32
    )
    forward_pair = section_map(driven, forward_coupling, section_len, forward_order)
    identity = (
        jnp.broadcast_to(
            jnp.eye(forward_pair[0].shape[1], dtype=jnp.float32), forward_pair[0].shape
        ),
        jnp.zeros_like(forward_pair[1]),
    )
    forward_in = prefix(forward_pair, "tm", compose, identity, False)[1]
    forward_states = resolve(forward_in, driven, forward_coupling, section_len, forward_order)
    partial_value = jnp.einsum(
        "trq,tfq->rf",
        forward_states.astype(jnp.bfloat16),
        arrow_rows,
        preferred_element_type=jnp.float32,
    )
    arrow_total = lax.psum(partial_value, ("tm", "space"))
    tip_state = jnp.dot(tip_side - arrow_total, tip_inverse.T, precision=lax.Precision.HIGHEST)
    tip_solution = jnp.dot(tip_state, tip_inverse, precision=lax.Precision.HIGHEST)
    arrow_wide = arrow_rows.astype(jnp.float32)
    backward_source = (
        forward_states
        - jnp.einsum("rf,tfq->trq", tip_solution, arrow_wide, precision=lax.Precision.HIGHEST)
    ).astype(jnp.bfloat16)
    spaces = lax.axis_size("space")
    place = lax.axis_index("space")
    share_width = diag_inverse.shape[1]

    def pass_down(step_index, carried):
        block_index = step_index + place - (spaces - 1)
        column_start = jnp.maximum(block_index, 0) * share_width
        columns = lax.dynamic_slice_in_dim(diag_inverse, column_start, share_width, 2)
        own_term = jnp.einsum(
            "trq,tqs->trs", backward_source, columns, preferred_element_type=jnp.float32
        )
        received = shifted(carried, "space", -1)
        return jnp.where(block_index >= 0, received + own_term, received)

    start_sum = jnp.zeros((slot_count, backward_source.shape[1], share_width), jnp.float32)
    sources = lax.fori_loop(0, spaces, pass_down, start_sum)
    backward_pair = section_map(sources, backward_coupling, section_len, backward_order)
    backward_in = prefix(backward_pair, "tm", compose, identity, True)[1]
    solution = resolve(backward_in, sources, backward_coupling, section_len, backward_order)
    return (solution, tip_solution)


def solution(mesh):
    placed = (
        P(),
        P("tm", None, None),
        P(),
        P("tm", "space", None),
        P("tm", "space", None),
        P("tm", "space", None),
        P("tm", None, "space"),
        P(),
    )
    return jax.shard_map(
        on_device,
        mesh=mesh,
        in_specs=placed,
        out_specs=(P("tm", None, "space"), P()),
        check_vma=False,
    )
```

profile of v0, /device:TPU:0, one launch (start us, length us, event | category | flops | bytes accessed | tf_op | source)
XLA Modules:
  0.0 244.5 jit_solution(15693550653643458159)
XLA Ops:
  7.2 1.3 dynamic_slice.42
  9.9 6.1 %fusion.95 = f32[4,64,512]{2,1,0:T(8,128)S(1)} fusion(bf16[4,64,2048]{2,1,0:T(8,128)(2,1)S(1)} %copy-done, bf16[4,512,2048]{2,1,0:T(8,128)(2,1)} %param.17), kind=kOutput, calls=%fused_computation.136 | convolution fusion | flops 536870912 | bytes 9961472 | tf_op jit(solution)/shard_map/trs,tqs->trq/dot_general | solution.py:99
  27.5 17.8 %all-gather.7.cloned.1.call-done = f32[8,64,512]{2,1,0:T(8,128)} async-done(((f32[1,64,512]{2,1,0:T(8,128)}), f32[8,64,512]{2,1,0:T(8,128)}) %all-gather.7.cloned.1.call-update) | async-done | bytes 1048592 | tf_op jit(solution)/shard_map/all_gather | solution.py:9
  45.3 30.4 %all-gather.11.cloned.1.call-done = f32[32,128,128]{2,1,0:T(8,128)} async-done(((f32[4,128,128]{2,1,0:T(8,128)}), f32[32,128,128]{2,1,0:T(8,128)}) %all-gather.11.cloned.1.call-update) | async-done | bytes 2097168 | tf_op jit(solution)/shard_map/all_gather | solution.py:9
  75.7 16.2 %while.44 = (s32[]{:T(128)}, f32[64,512]{1,0:T(8,128)S(1)}, s32[]{:T(128)}, f32[8,4,128,128]{3,2,1,0:T(8,128)}, f32[8,64,512]{2,1,0:T(8,128)}, /*index=5*/s32[]{:T(128)}, s32[]{:T(128)}) while((s32[]{:T(128)}, f32[64,512]{1,0:T(8,128)S(1)}, s32[]{:T(128)}, f32[8,4,128,128]{3,2,1,0:T(8,128)}, f32[8,64,512]{2,1,0:T(8,128)}, ...), condition=%wide.region_1.2_spmd.clone, body=%wide.region_0.1_spmd.clone.sunk | while | flops 50462720 | bytes 1049190 | solution.py:21
  78.0 1.3 convolution_bitcast_fusion.16
  84.9 1.4 convolution_bitcast_fusion.16
  89.6 1.3 convolution_bitcast_fusion.16
  95.7 40.3 %psum.7 = f32[64,8]{0,1:T(8,128)S(1)} all-reduce(f32[64,8]{0,1:T(8,128)S(1)} %convolution_bitcast_fusion.13), channel_id=1, replica_groups=mesh['tm'=8,'space'=4] {'tm','space'}, use_global_device_ids=true, to_apply=%region_2.3 | all-reduce | flops 512 | bytes 4096 | tf_op jit(solution)/shard_map/psum | solution.py:117
  136.3 1.4 fusion.25
  137.7 61.5 %while.45 = (s32[]{:T(128)}, f32[4,64,512]{2,1,0:T(8,128)S(1)}, s32[]{:T(128)}, bf16[4,512,2048]{2,1,0:T(8,128)(2,1)}, bf16[4,64,512]{2,1,0:T(8,128)(2,1)S(1)}, ...) while((s32[]{:T(128)}, f32[4,64,512]{2,1,0:T(8,128)S(1)}, s32[]{:T(128)}, ...), condition=%wide.region_4.5_spmd.clone, body=%wide.region_3.4_spmd.clone.sunk | while | flops 134610960 | bytes 6553847 | solution.py:140
  139.1 13.4 %collective-permute-done = f32[4,64,512]{2,1,0:T(8,128)S(1)} collective-permute-done((f32[4,64,512]{2,1,0:T(8,128)S(1)}, f32[4,64,512]{2,1,0:T(8,128)S(1)}, u32[]{:S(2)}, u32[]{:S(2)}) %collective-permute-start) | collective-permute-done | bytes 524320 | tf_op jit(solution)/shard_map/while/body/eval_jaxpr/ppermute | solution.py:27
  152.5 2.1 fusion.171
  155.9 12.2 %collective-permute-done = f32[4,64,512]{2,1,0:T(8,128)S(1)} collective-permute-done((f32[4,64,512]{2,1,0:T(8,128)S(1)}, f32[4,64,512]{2,1,0:T(8,128)S(1)}, u32[]{:S(2)}, u32[]{:S(2)}) %collective-permute-start) | collective-permute-done | bytes 524320 | tf_op jit(solution)/shard_map/while/body/eval_jaxpr/ppermute | solution.py:27
  168.2 2.1 fusion.171
  171.6 11.4 %collective-permute-done = f32[4,64,512]{2,1,0:T(8,128)S(1)} collective-permute-done((f32[4,64,512]{2,1,0:T(8,128)S(1)}, f32[4,64,512]{2,1,0:T(8,128)S(1)}, u32[]{:S(2)}, u32[]{:S(2)}) %collective-permute-start) | collective-permute-done | bytes 524320 | tf_op jit(solution)/shard_map/while/body/eval_jaxpr/ppermute | solution.py:27
  183.0 2.1 fusion.171
  186.5 10.6 %collective-permute-done = f32[4,64,512]{2,1,0:T(8,128)S(1)} collective-permute-done((f32[4,64,512]{2,1,0:T(8,128)S(1)}, f32[4,64,512]{2,1,0:T(8,128)S(1)}, u32[]{:S(2)}, u32[]{:S(2)}) %collective-permute-start) | collective-permute-done | bytes 524320 | tf_op jit(solution)/shard_map/while/body/eval_jaxpr/ppermute | solution.py:27
  197.1 2.1 fusion.171
  201.8 3.1 %rev.6 = f32[8,4,128,128]{3,2,1,0:T(8,128)} reverse(f32[8,4,128,128]{3,2,1,0:T(8,128)} %bitcast.289), dimensions={0} | reverse | bytes 4194304 | tf_op jit(solution)/shard_map/rev | solution.py:11
  204.9 18.9 %all-gather.9.cloned.1.call-done = f32[8,64,512]{2,1,0:T(8,128)} async-done(((f32[1,64,512]{2,1,0:T(8,128)}), f32[8,64,512]{2,1,0:T(8,128)}) %all-gather.9.cloned.1.call-update) | async-done | bytes 1048592 | tf_op jit(solution)/shard_map/all_gather | solution.py:9
  223.8 1.3 rev.7
  225.1 9.7 %while.46 = (s32[]{:T(128)}, f32[64,512]{1,0:T(8,128)S(1)}, s32[]{:T(128)}, f32[8,4,128,128]{3,2,1,0:T(8,128)}, f32[8,64,512]{2,1,0:T(8,128)S(1)}, /*index=5*/s32[]{:T(128)}, s32[]{:T(128)}) while((s32[]{:T(128)}, f32[64,512]{1,0:T(8,128)S(1)}, s32[]{:T(128)}, f32[8,4,128,128]{3,2,1,0:T(8,128)}, f32[8,64,512]{2,1,0:T(8,128)S(1)}, ...), condition=%wide.region_6.7_spmd.clone, body=%wide.region_5.6_spmd.clone.sunk | while | flops 50462720 | bytes 1049190 | solution.py:21
  225.2 1.3 convolution_bitcast_fusion.17
  (141 shorter events, 44.9 us)
Async XLA Ops:
  7.2 2.7 %copy-start = (bf16[4,64,2048]{2,1,0:T(8,128)(2,1)S(1)}, bf16[4,64,2048]{2,1,0:T(8,128)(2,1)}, u32[]{:S(2)}) copy-start(bf16[4,64,2048]{2,1,0:T(8,128)(2,1)} %param.15) | copy-start | bytes 3145732
  7.2 38.1 %all-gather.7.cloned.1.call-start = ((), (), s32[]{:S(2)}) async-start(), calls=%async_computation | async-start | bytes 1179648 | tf_op jit(solution)/shard_map/all_gather | solution.py:9
  9.9 6.3 %copy-start.4 = (bf16[4,512,128]{2,1,0:T(8,128)(2,1)S(1)}, bf16[4,512,128]{2,1,0:T(8,128)(2,1)}, u32[]{:S(2)}) copy-start(bf16[4,512,128]{2,1,0:T(8,128)(2,1)} %param.18) | copy-start | bytes 1572868
  20.4 55.3 %all-gather.11.cloned.1.call-start = ((), (), s32[]{:S(2)}) async-start(), calls=%async_computation.2 | async-start | bytes 2359296 | tf_op jit(solution)/shard_map/all_gather | solution.py:9
  22.8 179.1 %all-gather.13.cloned.1.call-start = ((), (), s32[]{:S(2)}) async-start(), calls=%async_computation.3 | async-start | bytes 2359296 | tf_op jit(solution)/shard_map/all_gather | solution.py:9
  26.2 197.6 %all-gather.9.cloned.1.call-start = ((), (), s32[]{:S(2)}) async-start(), calls=%async_computation.1 | async-start | bytes 1179648 | tf_op jit(solution)/shard_map/all_gather | solution.py:9
  26.7 49.0 %copy-start.1 = (f32[64,4,128]{2,0,1:T(8,128)}, f32[64,4,128]{2,0,1:T(8,128)S(1)}, u32[]{:S(2)}) copy-start(f32[64,4,128]{2,0,1:T(8,128)S(1)} %convolution_bitcast_fusion.7) | copy-start | bytes 393220
  93.5 42.5 %copy-start.6 = (f32[64,8]{0,1:T(8,128)S(1)}, f32[64,8]{0,1:T(8,128)}, u32[]{:S(2)}) copy-start(f32[64,8]{0,1:T(8,128)} %param.16) | copy-start | bytes 6148
  93.5 42.5 %copy-start.7 = (f32[8,8]{1,0:T(8,128)S(1)}, f32[8,8]{1,0:T(8,128)}, u32[]{:S(2)}) copy-start(f32[8,8]{1,0:T(8,128)} %param.21) | copy-start | bytes 772
  94.1 0.6 copy-start.5
  136.3 1.4 copy-start.8
  137.7 61.7 %copy-start.2 = (f32[64,4,128]{2,0,1:T(8,128)S(1)}, f32[64,4,128]{2,0,1:T(8,128)}, u32[]{:S(2)}) copy-start(f32[64,4,128]{2,0,1:T(8,128)} %copy-done.1) | copy-start | bytes 393220
  137.8 14.7 %collective-permute-start = (f32[4,64,512]{2,1,0:T(8,128)S(1)}, f32[4,64,512]{2,1,0:T(8,128)S(1)}, u32[]{:S(2)}, u32[]{:S(2)}) collective-permute-start(f32[4,64,512]{2,1,0:T(8,128)S(1)} %broadcast_select_fusion.2), channel_id=1, source_target_pairs={{1,0},{2,1},{3,2},{5,4},{6,5},{7,6},{9,8},{10,9},{11,10},{13,12},{... | collective-permute-start | bytes 1572872 | tf_op jit(solution)/shard_map/while/body/eval_jaxpr/ppermute | solution.py:27
  154.6 13.6 %collective-permute-start = (f32[4,64,512]{2,1,0:T(8,128)S(1)}, f32[4,64,512]{2,1,0:T(8,128)S(1)}, u32[]{:S(2)}, u32[]{:S(2)}) collective-permute-start(f32[4,64,512]{2,1,0:T(8,128)S(1)} %broadcast_select_fusion.2), channel_id=1, source_target_pairs={{1,0},{2,1},{3,2},{5,4},{6,5},{7,6},{9,8},{10,9},{11,10},{13,12},{... | collective-permute-start | bytes 1572872 | tf_op jit(solution)/shard_map/while/body/eval_jaxpr/ppermute | solution.py:27
  170.3 12.7 %collective-permute-start = (f32[4,64,512]{2,1,0:T(8,128)S(1)}, f32[4,64,512]{2,1,0:T(8,128)S(1)}, u32[]{:S(2)}, u32[]{:S(2)}) collective-permute-start(f32[4,64,512]{2,1,0:T(8,128)S(1)} %broadcast_select_fusion.2), channel_id=1, source_target_pairs={{1,0},{2,1},{3,2},{5,4},{6,5},{7,6},{9,8},{10,9},{11,10},{13,12},{... | collective-permute-start | bytes 1572872 | tf_op jit(solution)/shard_map/while/body/eval_jaxpr/ppermute | solution.py:27
  185.2 12.0 %collective-permute-start = (f32[4,64,512]{2,1,0:T(8,128)S(1)}, f32[4,64,512]{2,1,0:T(8,128)S(1)}, u32[]{:S(2)}, u32[]{:S(2)}) collective-permute-start(f32[4,64,512]{2,1,0:T(8,128)S(1)} %broadcast_select_fusion.2), channel_id=1, source_target_pairs={{1,0},{2,1},{3,2},{5,4},{6,5},{7,6},{9,8},{10,9},{11,10},{13,12},{... | collective-permute-start | bytes 1572872 | tf_op jit(solution)/shard_map/while/body/eval_jaxpr/ppermute | solution.py:27
  199.2 1.7 copy-start.3
Sparse Core Ops, SparseCore 0:
  20.5 24.7 all-gather.6
  46.9 28.7 all-gather.10
  77.9 28.5 all-gather.12
  201.9 21.8 all-gather.8
where the time goes:
time: 246 us; the launch traced here: 244 us
  waiting for transfers between devices  115 us (47%)
  matrix products  45.4 us (18%)
  blocking collectives  40.3 us (16%)
  between operations  17.1 us (7%)
  local copies, waits for them, and re-layouts  10.9 us (4%)
  other arithmetic  9.95 us (4%)
  starting transfers between devices  5.33 us (2%)
    all_gather x4, waiting for transfers between devices, prefix(): pieces = jax.tree.map(lambda part: lax.all_gather(part, axis), value)  67.1 us
    ppermute x4, waiting for transfers between devices, shifted(): lax.ppermute(value, axis, [(source, source + steps) for source in range(l...  47.7 us
    psum x1, blocking collectives, on_device(): arrow_total = lax.psum(partial_value, ('tm', 'space'))  40.3 us
    dot_general x14, matrix products, apply_map(): jnp.einsum('rni,nik->rnk', shaped, mapping, precision=lax.Precision.HIGHEST)  18.3 us
    dot_general x4, matrix products, pass_down(): jnp.einsum('trq,tqs->trs', backward_source, columns, preferred_element_ty...  8.22 us
    select_n x14, other arithmetic, lap(): jnp.where(position < mine, new, old)  7.11 us
    dot_general x1, matrix products, on_device(): jnp.einsum('trs,tqs->trq', right_side, diag_inverse, preferred_element_ty...  6.1 us
    dot_general x16, matrix products, couple(): jnp.einsum('rnk,nik->rni', shaped, blocks, precision=lax.Precision.HIGHEST)  5.59 us
  transfers between devices with their start and end apart: 8, of which 7 were waited for; matrix products, arithmetic and copies ran while one was open for 17% of the time, Pallas kernels for 0%

commit v1 on v0

v1 whole, which is shorter than its diff:
```python
import functools

import jax
import jax.numpy as jnp
from jax import lax
from jax.experimental import pallas as pl
from jax.experimental.pallas import tpu as pltpu
from jax.sharding import PartitionSpec as P

F32 = jnp.float32
BF16 = jnp.bfloat16
MESH = pl.DeviceIdType.MESH


def dot(a, b, contract):
    return lax.dot_general(a, b, (contract, ((), ())), preferred_element_type=F32)


def stacked(x):
    high = x.astype(BF16).astype(F32)
    return jnp.concatenate([high, x - high], 0).astype(BF16)


def folded(y):
    rows = y.shape[0] // 2
    return y[:rows] + y[rows:]


def couple(x, block):
    return folded(dot(stacked(x), block, ((1,), (1,))))


def apply_map(x, high, low):
    rows = x.shape[0]
    pieces = stacked(x)
    return folded(dot(pieces, high, ((1,), (0,)))) + dot(pieces[:rows], low, ((1,), (0,)))


def kernel(
    n_tm, n_sp, sec, rs, tip_side, diag_hbm, fc, bc, arrow, tip_inv,
    sol, tip_out,
    diag, fmap_h, fmap_l, bmap_h, bmap_l, driven, f_in, f_out, f_split,
    w_send, w_recv, v_send, v_recv, g_loc, b_in, b_out, part, gath_sp, gath_tm, mine_tm,
    diag_sem, fs_sem, fr_sem, bs_sem, br_sem, ws_sem, wr_sem, vs_sem, vr_sem,
    as_sem, ar_sem, ts_sem, tr_sem,
):
    T, rows = rs.shape[0], rs.shape[1]
    width, sub = fc.shape[1], fc.shape[2]
    nsub = width // sub
    F = arrow.shape[1]
    s, p = lax.axis_index("tm"), lax.axis_index("space")
    length = sec[s]

    loads = [
        pltpu.make_async_copy(diag_hbm.at[t], diag.at[t], diag_sem.at[t]) for t in range(T)
    ]
    for load in loads:
        load.start()

    barrier = pltpu.get_barrier_semaphore()
    for d in range(1, n_tm):
        pl.semaphore_signal(barrier, inc=1, device_id={"tm": lax.rem(s + d, n_tm)}, device_id_type=MESH)
    for d in range(1, n_sp):
        pl.semaphore_signal(barrier, inc=1, device_id={"space": lax.rem(p + d, n_sp)}, device_id_type=MESH)

    def cols(n):
        return slice(n * sub, (n + 1) * sub)

    def select(t, new, old):
        if t == 0:
            return new
        return jnp.where(jnp.full(new.shape, length, jnp.int32) > t, new, old)

    def remote(src, dst, send, recv, to):
        return pltpu.make_async_remote_copy(
            src_ref=src, dst_ref=dst, send_sem=send, recv_sem=recv, device_id=to, device_id_type=MESH
        )

    def section_maps(coupling, order, high_ref, low_ref):
        row = lax.broadcasted_iota(jnp.int32, (sub, sub), 0)
        col = lax.broadcasted_iota(jnp.int32, (sub, sub), 1)
        eye = jnp.where(row == col, 1.0, 0.0).astype(F32)
        maps = [eye] * nsub
        for t in order:
            for n in range(nsub):
                maps[n] = select(t, -couple(maps[n], coupling[t, cols(n), :]), maps[n])
                high = maps[n].astype(BF16)
                high_ref[n, :, cols(t)] = high
                low_ref[n, :, cols(t)] = (maps[n] - high.astype(F32)).astype(BF16)

    section_maps(fc, range(T), fmap_h, fmap_l)
    carry = [None] * nsub
    for t in range(T):
        loads[t].wait()
        full = dot(rs[t], diag[t], ((1,), (1,)))
        for n in range(nsub):
            new = full[:, cols(n)]
            if t > 0:
                new = select(t, new - couple(carry[n], fc[t, cols(n), :]), carry[n])
            carry[n] = new
            driven[t, n] = new

    pl.semaphore_wait(barrier, n_tm - 1 + n_sp - 1)

    def arrow_products():
        for q in range(n_sp - 1):

            @pl.when(p > q)
            def _():
                for t in range(T):
                    full = dot(arrow[t], diag[t, :, q * width : (q + 1) * width], ((1,), (0,)))
                    for n in range(nsub):
                        v_send[q, t, n] = full[:, cols(n)]
                remote(v_send.at[q], v_recv.at[p - 1], vs_sem.at[q], vr_sem.at[p - 1], {"space": q}).start()

    def early():
        arrow_products()
        section_maps(bc, range(T - 1, -1, -1), bmap_h, bmap_l)

    pl.when(s >= n_tm // 2)(early)

    def chain(first, last, to, arrived, leaving, ssem, rsem, own, high, low, at):
        @pl.when(first)
        def _():
            arrived[...] = jnp.zeros(arrived.shape, F32)

        for n in range(nsub):
            hop = remote(leaving.at[n], arrived.at[n], ssem.at[n], rsem.at[n], {"tm": to})
            pl.when(jnp.logical_not(first))(hop.wait_recv)

            @pl.when(jnp.logical_not(last))
            def _():
                leaving[n] = own[at, n] + apply_map(
                    arrived[n], high[n, :, cols(at)], low[n, :, cols(at)]
                )
                hop.start()

    def chain_end(last, to, arrived, leaving, ssem, rsem):
        @pl.when(jnp.logical_not(last))
        def _():
            for n in range(nsub):
                remote(leaving.at[n], arrived.at[n], ssem.at[n], rsem.at[n], {"tm": to}).wait_send()

    f_first, f_last, f_to = s == 0, s == n_tm - 1, lax.rem(s + 1, n_tm)
    chain(f_first, f_last, f_to, f_in, f_out, fs_sem, fr_sem, driven, fmap_h, fmap_l, T - 1)

    for n in range(nsub):
        states = apply_map(f_in[n], fmap_h[n], fmap_l[n])
        for t in range(T):
            state = driven[t, n] + states[:, cols(t)]
            state = select(t, state, jnp.zeros_like(state))
            f_split[t, :, cols(n)] = stacked(state)

    for q in range(n_sp - 1):

        @pl.when(p > q)
        def _():
            for t in range(T - 1, -1, -1):
                full = folded(dot(f_split[t], diag[t, :, q * width : (q + 1) * width], ((1,), (0,))))
                for n in range(nsub):
                    w_send[q, t, n] = full[:, cols(n)]
                remote(
                    w_send.at[q, t], w_recv.at[p - 1, t], ws_sem.at[q, t], wr_sem.at[p - 1, t], {"space": q}
                ).start()

    total = jnp.zeros((F, 2 * rows), F32)
    for t in range(T):
        total = total + dot(arrow[t], f_split[t], ((1,), (1,)))
    part[...] = total
    gath_sp[p] = total
    for d in range(1, n_sp):
        remote(part, gath_sp.at[p], as_sem.at[d - 1], ar_sem.at[p], {"space": lax.rem(p + d, n_sp)}).start()

    pl.when(s < n_tm // 2)(early)

    for d in range(1, n_sp):
        come = lax.rem(p + d, n_sp)
        remote(part, gath_sp.at[come], as_sem.at[d - 1], ar_sem.at[come], {"space": come}).wait_recv()
    total = gath_sp[0]
    for i in range(1, n_sp):
        total = total + gath_sp[i]
    mine_tm[...] = total
    gath_tm[s] = total
    for d in range(1, n_tm):
        remote(mine_tm, gath_tm.at[s], ts_sem.at[d - 1], tr_sem.at[s], {"tm": lax.rem(s + d, n_tm)}).start()

    own_cols = pl.ds(pl.multiple_of(p * width, width), width)
    for t in range(T):
        block = diag[t, :, own_cols]
        full = folded(dot(f_split[t], block, ((1,), (0,))))
        arrow_full = dot(arrow[t], block, ((1,), (0,)))
        for n in range(nsub):
            g_loc[t, n, :rows] = full[:, cols(n)]
            g_loc[t, n, rows:] = arrow_full[:, cols(n)]
    for q in range(1, n_sp):

        @pl.when(p < q)
        def _():
            remote(v_send.at[0], v_recv.at[q - 1], vs_sem.at[0], vr_sem.at[q - 1], {"space": q}).wait_recv()
            for t in range(T):
                for n in range(nsub):
                    g_loc[t, n, rows:] += v_recv[q - 1, t, n]

    for t in range(T - 1, -1, -1):
        for q in range(1, n_sp):

            @pl.when(p < q)
            def _():
                remote(
                    w_send.at[0, t], w_recv.at[q - 1, t], ws_sem.at[0, t], wr_sem.at[q - 1, t], {"space": q}
                ).wait_recv()
                for n in range(nsub):
                    g_loc[t, n, :rows] += w_recv[q - 1, t, n]

        for n in range(nsub):
            new = g_loc[t, n]
            if t < T - 1:
                old = g_loc[t + 1, n]
                new = select(t, new - couple(old, bc[t, cols(n), :]), old)
            else:
                new = select(t, new, jnp.zeros_like(new))
            g_loc[t, n] = new

    b_first, b_last, b_to = s == n_tm - 1, s == 0, lax.rem(s + n_tm - 1, n_tm)
    chain(b_first, b_last, b_to, b_in, b_out, bs_sem, br_sem, g_loc, bmap_h, bmap_l, 0)

    for d in range(1, n_tm):
        come = lax.rem(s + d, n_tm)
        remote(mine_tm, gath_tm.at[come], ts_sem.at[d - 1], tr_sem.at[come], {"tm": come}).wait_recv()
    total = gath_tm[0]
    for i in range(1, n_tm):
        total = total + gath_tm[i]
    exact = functools.partial(
        lax.dot_general, preferred_element_type=F32, precision=lax.Precision.HIGHEST
    )
    side = tip_side[...] - total.T[:rows, :]
    tip_state = exact(side, tip_inv[...], (((1,), (1,)), ((), ())))
    tip = exact(tip_state, tip_inv[...], (((1,), (0,)), ((), ())))
    tip_out[...] = tip

    for n in range(nsub):
        states = apply_map(b_in[n], bmap_h[n], bmap_l[n])
        for t in range(T):
            state = g_loc[t, n] + states[:, cols(t)]
            value = state[:rows] - exact(tip, state[rows:], (((1,), (0,)), ((), ())))
            sol[t, :, cols(n)] = select(t, value, jnp.zeros_like(value))

    chain_end(f_last, f_to, f_in, f_out, fs_sem, fr_sem)
    chain_end(b_last, b_to, b_in, b_out, bs_sem, br_sem)
    for q in range(n_sp - 1):

        @pl.when(p > q)
        def _():
            remote(v_send.at[q], v_recv.at[p - 1], vs_sem.at[q], vr_sem.at[p - 1], {"space": q}).wait_send()
            for t in range(T):
                remote(
                    w_send.at[q, t], w_recv.at[p - 1, t], ws_sem.at[q, t], wr_sem.at[p - 1, t], {"space": q}
                ).wait_send()

    for d in range(1, n_sp):
        remote(part, gath_sp.at[p], as_sem.at[d - 1], ar_sem.at[p], {"space": lax.rem(p + d, n_sp)}).wait_send()
    for d in range(1, n_tm):
        remote(mine_tm, gath_tm.at[s], ts_sem.at[d - 1], tr_sem.at[s], {"tm": lax.rem(s + d, n_tm)}).wait_send()


def on_device(n_tm, n_sp, sections, right_side, tip_side, diag_inverse, fwd, bwd, arrow_rows, tip_inverse):
    T, rows, total_width = right_side.shape
    width, sub = fwd.shape[1], fwd.shape[2]
    nsub = width // sub
    F = arrow_rows.shape[1]
    both = rows + F
    vmem = pl.BlockSpec(memory_space=pltpu.VMEM)
    maps = pltpu.VMEM((nsub, sub, T * sub), BF16)
    dma = pltpu.SemaphoreType.DMA
    others = n_sp - 1
    return pl.pallas_call(
        functools.partial(kernel, n_tm, n_sp),
        out_shape=(
            jax.ShapeDtypeStruct((T, rows, width), F32),
            jax.ShapeDtypeStruct(tip_side.shape, F32),
        ),
        in_specs=[
            pl.BlockSpec(memory_space=pltpu.SMEM),
            vmem,
            vmem,
            pl.BlockSpec(memory_space=pl.ANY),
            vmem,
            vmem,
            vmem,
            vmem,
        ],
        out_specs=(vmem, vmem),
        scratch_shapes=[
            pltpu.VMEM(diag_inverse.shape, BF16),
            maps,
            maps,
            maps,
            maps,
            pltpu.VMEM((T, nsub, rows, sub), F32),
            pltpu.VMEM((nsub, rows, sub), F32),
            pltpu.VMEM((nsub, rows, sub), F32),
            pltpu.VMEM((T, 2 * rows, width), BF16),
            pltpu.VMEM((others, T, nsub, rows, sub), F32),
            pltpu.VMEM((others, T, nsub, rows, sub), F32),
            pltpu.VMEM((others, T, nsub, F, sub), F32),
            pltpu.VMEM((others, T, nsub, F, sub), F32),
            pltpu.VMEM((T, nsub, both, sub), F32),
            pltpu.VMEM((nsub, both, sub), F32),
            pltpu.VMEM((nsub, both, sub), F32),
            pltpu.VMEM((F, 2 * rows), F32),
            pltpu.VMEM((n_sp, F, 2 * rows), F32),
            pltpu.VMEM((n_tm, F, 2 * rows), F32),
            pltpu.VMEM((F, 2 * rows), F32),
            dma((T,)),
            dma((nsub,)),
            dma((nsub,)),
            dma((nsub,)),
            dma((nsub,)),
            dma((others, T)),
            dma((others, T)),
            dma((others,)),
            dma((others,)),
            dma((others,)),
            dma((n_sp,)),
            dma((n_tm - 1,)),
            dma((n_tm,)),
        ],
        compiler_params=pltpu.CompilerParams(
            collective_id=0, has_side_effects=True, vmem_limit_bytes=56 * 1024 * 1024
        ),
        cost_estimate=pl.CostEstimate(
            flops=8 * T * rows * width * total_width, bytes_accessed=2 * diag_inverse.size, transcendentals=0
        ),
    )(sections, right_side, tip_side, diag_inverse, fwd, bwd, arrow_rows, tip_inverse)


def solution(mesh):
    placed = (
        P(),
        P("tm", None, None),
        P(),
        P("tm", "space", None),
        P("tm", "space", None),
        P("tm", "space", None),
        P("tm", None, "space"),
        P(),
    )
    return jax.shard_map(
        functools.partial(on_device, mesh.shape["tm"], mesh.shape["space"]),
        mesh=mesh,
        in_specs=placed,
        out_specs=(P("tm", None, "space"), P()),
        check_vma=False,
    )
```

time: 246 us -> 71.4 us (0.29)
  waiting for transfers between devices: 115 us -> 0 us
  Pallas kernels: 0 us -> 65.8 us
  matrix products: 45.4 us -> 0 us
  blocking collectives: 40.3 us -> 0 us
  between operations: 17.1 us -> 0.64 us
  other arithmetic: 9.95 us -> 0 us
  local copies, waits for them, and re-layouts: 10.9 us -> 4.67 us
  starting transfers between devices: 5.33 us -> 0 us
    all_gather x4 -> x0, waiting for transfers between devices: 67.1 us -> none  [prefix(): pieces = jax.tree.map(lambda part: lax.all_gather(part, axis), value)]
    pallas_call x0 -> x1, Pallas kernels: none -> 65.8 us  [on_device(): pl.pallas_call(functools.partial(kernel, n_tm, n_sp), out_shape=(jax.Shap...]
    ppermute x4 -> x0, waiting for transfers between devices: 47.7 us -> none  [shifted(): lax.ppermute(value, axis, [(source, source + steps) for source in range(l...]
    dot_general x47 -> x0, matrix products: 45.4 us -> none  [the longest x14 18.3 us: apply_map(): jnp.einsum('rni,nik->rnk', shaped, mapping, precision=lax.Precision.HIGHEST)]
    psum x1 -> x0, blocking collectives: 40.3 us -> none  [on_device(): arrow_total = lax.psum(partial_value, ('tm', 'space'))]
    select_n x22 -> x0, other arithmetic: 8.94 us -> none  [the longest x14 7.11 us: lap(): jnp.where(position < mine, new, old)]
    ppermute x4 -> x0, starting transfers between devices: 5.17 us -> none  [shifted(): lax.ppermute(value, axis, [(source, source + steps) for source in range(l...]
    rev x2 -> x0, local copies, waits for them, and re-layouts: 4.44 us -> none  [prefix(): pieces = jax.tree.map(lambda part: part[::-1], pieces)]
  transfers between devices with their start and end apart: 8 -> 0, of which waited for: 7 -> 0; matrix products, arithmetic and copies ran while one was open for 17% -> 0% of each run, Pallas kernels for 0% -> 0%
where the time goes in v1:
time: 71.4 us; the launch traced here: 71.1 us
  Pallas kernels  65.8 us (92%)
  local copies, waits for them, and re-layouts  4.67 us (7%)
    pallas_call x1, Pallas kernels, on_device(): pl.pallas_call(functools.partial(kernel, n_tm, n_sp), out_shape=(jax.Shap...  65.8 us
    unnamed x2, local copies, waits for them, and re-layouts  3.25 us

profile of v1, /device:TPU:0, one launch (start us, length us, event | category | flops | bytes accessed | tf_op | source)
XLA Modules:
  0.0 71.1 jit_solution(17173861383188474045)
XLA Ops:
  0.6 1.4 %copy.10.tip_side = f32[64,8]{1,0:T(8,128)} copy(f32[64,8]{0,1:T(8,128)} %param.10) | data formatting | bytes 4096 | tf_op args[2]
  2.0 65.8 %shard_map.95 = (f32[4,64,512]{2,1,0:T(8,128)}, f32[64,8]{1,0:T(8,128)}) custom-call(s32[8]{0:T(128)} %sec.1, bf16[4,64,2048]{2,1,0:T(8,128)(2,1)} %rs.1, f32[64,8]{1,0:T(8,128)} %copy.10.tip_side, bf16[4,512,2048]{2,1,0:T(8,128)(2,1)} %diag_hbm.1, bf16[4,512,128]{2,1,0:T(8,128)(2,1)} %fc.1, bf16[4,512,128]{2,1,0:T(8,128)(2,1)} %bc.1, ...), custom_call_target="tpu_custom_call" | custom-call | flops 2147483648 | bytes 8388608 | tf_op jit(solution)/shard_map/pallas_call | solution.py:276
  67.8 1.4 %copy.11 = f32[64,8]{0,1:T(8,128)} copy(f32[64,8]{1,0:T(8,128)} %get-tuple-element.3) | data formatting | bytes 4096 | tf_op jit(solution)/shard_map/pallas_call | solution.py:276
  69.2 1.9 %copy.13 = f32[4,64,512]{2,1,0:T(8,128)} copy(f32[4,64,512]{2,1,0:T(8,128)} %get-tuple-element.6) | data formatting | bytes 1048576

commit v2 on v1

v2 whole, which is shorter than its diff:
```python
import functools

import jax
import jax.numpy as jnp
from jax import lax
from jax.experimental import pallas as pl
from jax.experimental.pallas import tpu as pltpu
from jax.sharding import PartitionSpec as P

F32 = jnp.float32
BF16 = jnp.bfloat16
MESH = pl.DeviceIdType.MESH


def dot(a, b, contract):
    return lax.dot_general(a, b, (contract, ((), ())), preferred_element_type=F32)


def stacked(x):
    high = x.astype(BF16).astype(F32)
    return jnp.concatenate([high, x - high], 0).astype(BF16)


def folded(y):
    rows = y.shape[0] // 2
    return y[:rows] + y[rows:]


def couple(x, block):
    return folded(dot(stacked(x), block, ((1,), (1,))))


def apply_map(x, high, low):
    rows = x.shape[0]
    pieces = stacked(x)
    return folded(dot(pieces, high, ((1,), (0,)))) + dot(pieces[:rows], low, ((1,), (0,)))


def kernel(
    n_tm, n_sp, sec, rs, tip_side, diag_hbm, fc, bc, arrow, tip_inv,
    sol, tip_out,
    diag, fmap_h, fmap_l, bmap_h, bmap_l, driven, f_split, g_loc,
    w_send, w_recv, w_pass, v_send, v_recv, part, gath_sp, gath_tm, mine_tm,
    f_scan, b_scan,
    diag_sem, ws_sem, wr_sem, ps_sem, pr_sem, vs_sem, vr_sem, as_sem, ar_sem, ts_sem, tr_sem,
):
    T, rows = rs.shape[0], rs.shape[1]
    width, sub = fc.shape[1], fc.shape[2]
    nsub = width // sub
    F = arrow.shape[1]
    s, p = lax.axis_index("tm"), lax.axis_index("space")
    core, chip, chips = lax.rem(s, 2), s // 2, n_tm // 2
    length = sec[s]
    half, split = (nsub // 2, True) if nsub % 2 == 0 else (nsub, False)
    base = core * half if split else 0
    other_base = half - core * half if split else 0
    mate = s + 1 - 2 * core

    loads = [
        pltpu.make_async_copy(diag_hbm.at[t], diag.at[t], diag_sem.at[t]) for t in range(T)
    ]
    for load in loads:
        load.start()

    barrier = pltpu.get_barrier_semaphore()
    for d in range(1, n_tm):
        pl.semaphore_signal(barrier, inc=1, device_id={"tm": lax.rem(s + d, n_tm)}, device_id_type=MESH)
    for d in range(1, n_sp):
        pl.semaphore_signal(barrier, inc=1, device_id={"space": lax.rem(p + d, n_sp)}, device_id_type=MESH)

    def cols(n):
        return slice(n * sub, (n + 1) * sub)

    def select(t, new, old):
        if t == 0:
            return new
        return jnp.where(jnp.full(new.shape, length, jnp.int32) > t, new, old)

    def remote(src, dst, send, recv, to):
        return pltpu.make_async_remote_copy(
            src_ref=src, dst_ref=dst, send_sem=send, recv_sem=recv, device_id=to, device_id_type=MESH
        )

    def section_maps(coupling, order, high_ref, low_ref, own_map):
        row = lax.broadcasted_iota(jnp.int32, (sub, sub), 0)
        col = lax.broadcasted_iota(jnp.int32, (sub, sub), 1)
        eye = jnp.where(row == col, 1.0, 0.0).astype(F32)
        maps = [eye] * nsub
        for t in order:
            for n in range(nsub):
                maps[n] = select(t, -couple(maps[n], coupling[t, cols(n), :]), maps[n])
                high = maps[n].astype(BF16)
                high_ref[n, :, cols(t)] = high
                low_ref[n, :, cols(t)] = (maps[n] - high.astype(F32)).astype(BF16)
        for n in range(nsub):
            own_map[n] = maps[n]

    def in_order(mine, theirs, lead):
        ahead = jnp.full(mine.shape, core, jnp.int32) == lead
        return jnp.where(ahead, mine, theirs), jnp.where(ahead, theirs, mine)

    def map_copy(scan):
        return remote(
            scan["map"].at[pl.ds(other_base, half)], scan["mate_map"],
            scan["sem"].at[0, 0], scan["sem"].at[1, 0], {"tm": mate},
        )

    def off_copy(scan, own):
        return remote(
            own.at[pl.ds(other_base, half)], scan["mate_off"],
            scan["sem"].at[0, 1], scan["sem"].at[1, 1], {"tm": mate},
        )

    def join_maps(scan, lead):
        map_copy(scan).wait_recv()
        for j in range(half):
            one, two = in_order(scan["map"][base + j], scan["mate_map"][j], lead)
            high = two.astype(BF16)
            both = apply_map(one, high, (two - high.astype(F32)).astype(BF16))
            for i, value in enumerate((both, one)):
                high = value.astype(BF16)
                scan["join_h"][j, :, cols(i)] = high
                scan["join_l"][j, :, cols(i)] = (value - high.astype(F32)).astype(BF16)
            scan["two"][j] = two

    def join_offsets(scan, own, lead):
        off_copy(scan, own).wait_recv()
        for j in range(half):
            one, two = in_order(own[base + j], scan["mate_off"][j], lead)
            after = scan["two"][j]
            high = after.astype(BF16)
            scan["join_off"][j, :, cols(0)] = two + apply_map(one, high, (after - high.astype(F32)).astype(BF16))
            scan["join_off"][j, :, cols(1)] = one

    def hop_copy(scan, j, to):
        return remote(
            scan["out"].at[j], scan["arrived"].at[j],
            scan["sem"].at[0, 2 + j], scan["sem"].at[1, 2 + j], {"tm": to},
        )

    def hand_copy(scan, j, at):
        return remote(
            scan["hand"].at[j], scan["into"].at[at + j],
            scan["sem"].at[0, 2 + half + j], scan["sem"].at[1, 2 + half + j], {"tm": mate},
        )

    def chain(scan, first, last, to, lead):
        @pl.when(first)
        def _():
            scan["arrived"][...] = jnp.zeros(scan["arrived"].shape, F32)

        for j in range(half):
            pl.when(jnp.logical_not(first))(hop_copy(scan, j, to).wait_recv)
            arrived = scan["arrived"][j]
            after = scan["join_off"][j] + apply_map(arrived, scan["join_h"][j], scan["join_l"][j])
            scan["out"][j] = after[:, :sub]
            pl.when(jnp.logical_not(last))(hop_copy(scan, j, to).start)
            mine, theirs = in_order(arrived, after[:, sub:], lead)
            scan["into"][base + j] = mine
            if split:
                scan["hand"][j] = theirs
                hand_copy(scan, j, base).start()
        if split:
            for j in range(half):
                hand_copy(scan, j, other_base).wait_recv()

    def scan_end(scan, own, last, to):
        map_copy(scan).wait_send()
        off_copy(scan, own).wait_send()
        for j in range(half):
            pl.when(jnp.logical_not(last))(hop_copy(scan, j, to).wait_send)
            if split:
                hand_copy(scan, j, base).wait_send()

    f_first, f_last, f_to = chip == 0, chip == chips - 1, lax.rem(s + 2, n_tm)
    b_first, b_last, b_to = f_last, f_first, lax.rem(s + n_tm - 2, n_tm)

    section_maps(fc, range(T), fmap_h, fmap_l, f_scan["map"])
    pl.semaphore_wait(barrier, n_tm - 1 + n_sp - 1)
    map_copy(f_scan).start()
    carry = [None] * nsub
    for t in range(T):
        loads[t].wait()
        full = dot(rs[t], diag[t], ((1,), (1,)))
        for n in range(nsub):
            new = full[:, cols(n)]
            if t > 0:
                new = select(t, new - couple(carry[n], fc[t, cols(n), :]), carry[n])
            carry[n] = new
            driven[t, n] = new
    off_copy(f_scan, driven.at[T - 1]).start()
    join_maps(f_scan, 0)
    join_offsets(f_scan, driven.at[T - 1], 0)

    def early():
        section_maps(bc, range(T - 1, -1, -1), bmap_h, bmap_l, b_scan["map"])
        map_copy(b_scan).start()
        for q in range(n_sp - 1):

            @pl.when(p > q)
            def _():
                for t in range(T):
                    full = dot(arrow[t], diag[t, :, q * width : (q + 1) * width], ((1,), (0,)))
                    for n in range(nsub):
                        v_send[q, t, n] = full[:, cols(n)]
                remote(v_send.at[q], v_recv.at[p - 1], vs_sem.at[q], vr_sem.at[p - 1], {"space": q}).start()

    pl.when(chip >= chips // 2)(early)

    chain(f_scan, f_first, f_last, f_to, 0)

    for n in range(nsub):
        states = apply_map(f_scan["into"][n], fmap_h[n], fmap_l[n])
        for t in range(T):
            state = driven[t, n] + states[:, cols(t)]
            state = select(t, state, jnp.zeros_like(state))
            f_split[t, :, cols(n)] = stacked(state)

    down = range(T - 1, -1, -1)
    merging = n_sp == 4 and nsub % 2 == 0
    mid = nsub // 2

    def product(q, t):
        full = folded(dot(f_split[t], diag[t, :, q * width : (q + 1) * width], ((1,), (0,))))
        for n in range(nsub):
            w_send[q, t, n] = full[:, cols(n)]

    def piece(h):
        return pl.ds(0, nsub) if h is None else pl.ds(h * mid, mid)

    def final(q, t, slot, h):
        sem = h or 0
        return remote(
            w_send.at[q, t, piece(h)], w_recv.at[slot, t, piece(h)],
            ws_sem.at[q, t, sem], wr_sem.at[slot, t, sem], {"space": q},
        )

    def passing(q, t, to, h):
        return remote(
            w_send.at[q, t, piece(h)], w_pass.at[t, piece(h)],
            ps_sem.at[t, h or 0], pr_sem.at[t], {"space": to},
        )

    def merge(q, t, h):
        passing(q, t, 0, h).wait_recv()
        for n in range(nsub) if h is None else range(h * mid, h * mid + mid):
            w_send[q, t, n] += w_pass[t, n]

    if merging:

        @pl.when(p == 3)
        def _():
            for t in down:
                product(0, t)
                passing(0, t, 2, 0).start()
                passing(0, t, 1, 1).start()
            for t in down:
                product(2, t)
                final(2, t, 0, None).start()
                product(1, t)
                merge(1, t, None)
                final(1, t, 0, None).start()

        @pl.when(p == 2)
        def _():
            for t in down:
                product(1, t)
                passing(1, t, 3, None).start()
                product(0, t)
                final(0, t, 1, 1).start()
            for t in down:
                merge(0, t, 0)
                final(0, t, 1, 0).start()

        @pl.when(p == 1)
        def _():
            for t in down:
                product(0, t)
                final(0, t, 0, 0).start()
            for t in down:
                merge(0, t, 1)
                final(0, t, 0, 1).start()

    else:
        for q in range(n_sp - 1):

            @pl.when(p > q)
            def _():
                for t in down:
                    product(q, t)
                    final(q, t, p - 1, None).start()

    total = jnp.zeros((F, 2 * rows), F32)
    for t in range(T):
        total = total + dot(arrow[t], f_split[t], ((1,), (1,)))
    part[...] = total
    gath_sp[p] = total
    for d in range(1, n_sp):
        remote(part, gath_sp.at[p], as_sem.at[d - 1], ar_sem.at[p], {"space": lax.rem(p + d, n_sp)}).start()

    pl.when(chip < chips // 2)(early)
    join_maps(b_scan, 1)

    own_cols = pl.ds(pl.multiple_of(p * width, width), width)
    for t in range(T):
        block = diag[t, :, own_cols]
        full = folded(dot(f_split[t], block, ((1,), (0,))))
        arrow_full = dot(arrow[t], block, ((1,), (0,)))
        for n in range(nsub):
            g_loc[t, n, :rows] = full[:, cols(n)]
            g_loc[t, n, rows:] = arrow_full[:, cols(n)]

    for d in range(1, n_sp):
        come = lax.rem(p + d, n_sp)
        remote(part, gath_sp.at[come], as_sem.at[d - 1], ar_sem.at[come], {"space": come}).wait_recv()
    total = gath_sp[0]
    for i in range(1, n_sp):
        total = total + gath_sp[i]
    mine_tm[...] = total
    gath_tm[s] = total
    for d in range(1, n_tm):
        remote(mine_tm, gath_tm.at[s], ts_sem.at[d - 1], tr_sem.at[s], {"tm": lax.rem(s + d, n_tm)}).start()

    for q in range(1, n_sp):

        @pl.when(p < q)
        def _():
            remote(v_send.at[0], v_recv.at[q - 1], vs_sem.at[0], vr_sem.at[q - 1], {"space": q}).wait_recv()
            for t in range(T):
                for n in range(nsub):
                    g_loc[t, n, rows:] += v_recv[q - 1, t, n]

    def take(t, slot, parts):
        for h in parts:
            final(0, t, slot, h).wait_recv()
        for n in range(nsub):
            g_loc[t, n, :rows] += w_recv[slot, t, n]

    for t in down:
        if merging:

            @pl.when(p == 0)
            def _():
                take(t, 0, (0, 1))
                take(t, 1, (0, 1))

            @pl.when(jnp.logical_or(p == 1, p == 2))
            def _():
                take(t, 0, (None,))

        else:
            for q in range(1, n_sp):
                pl.when(p < q)(functools.partial(take, t, q - 1, (None,)))

        for n in range(nsub):
            new = g_loc[t, n]
            if t < T - 1:
                old = g_loc[t + 1, n]
                new = select(t, new - couple(old, bc[t, cols(n), :]), old)
            else:
                new = select(t, new, jnp.zeros_like(new))
            g_loc[t, n] = new

    off_copy(b_scan, g_loc.at[0]).start()
    join_offsets(b_scan, g_loc.at[0], 1)
    chain(b_scan, b_first, b_last, b_to, 1)

    for d in range(1, n_tm):
        come = lax.rem(s + d, n_tm)
        remote(mine_tm, gath_tm.at[come], ts_sem.at[d - 1], tr_sem.at[come], {"tm": come}).wait_recv()
    total = gath_tm[0]
    for i in range(1, n_tm):
        total = total + gath_tm[i]
    exact = functools.partial(
        lax.dot_general, preferred_element_type=F32, precision=lax.Precision.HIGHEST
    )
    side = tip_side[...] - total[:, :rows]
    tip_state = exact(tip_inv[...], side, (((1,), (0,)), ((), ())))
    turned = exact(tip_inv[...].T, tip_state, (((1,), (0,)), ((), ())))
    tip_out[...] = turned
    tip = turned.T

    for n in range(nsub):
        states = apply_map(b_scan["into"][n], bmap_h[n], bmap_l[n])
        for t in range(T):
            state = g_loc[t, n] + states[:, cols(t)]
            value = state[:rows] - exact(tip, state[rows:], (((1,), (0,)), ((), ())))
            sol[t, :, cols(n)] = select(t, value, jnp.zeros_like(value))

    scan_end(f_scan, driven.at[T - 1], f_last, f_to)
    scan_end(b_scan, g_loc.at[0], b_last, b_to)
    for q in range(n_sp - 1):

        @pl.when(p > q)
        def _():
            remote(v_send.at[q], v_recv.at[p - 1], vs_sem.at[q], vr_sem.at[p - 1], {"space": q}).wait_send()
            if not merging:
                for t in down:
                    final(q, t, p - 1, None).wait_send()

    if merging:

        @pl.when(p == 3)
        def _():
            for t in down:
                passing(0, t, 2, 0).wait_send()
                passing(0, t, 1, 1).wait_send()
                final(2, t, 0, None).wait_send()
                final(1, t, 0, None).wait_send()

        @pl.when(p == 2)
        def _():
            for t in down:
                passing(1, t, 3, None).wait_send()
                final(0, t, 1, 0).wait_send()
                final(0, t, 1, 1).wait_send()

        @pl.when(p == 1)
        def _():
            for t in down:
                final(0, t, 0, 0).wait_send()
                final(0, t, 0, 1).wait_send()

    for d in range(1, n_sp):
        remote(part, gath_sp.at[p], as_sem.at[d - 1], ar_sem.at[p], {"space": lax.rem(p + d, n_sp)}).wait_send()
    for d in range(1, n_tm):
        remote(mine_tm, gath_tm.at[s], ts_sem.at[d - 1], tr_sem.at[s], {"tm": lax.rem(s + d, n_tm)}).wait_send()


def scan_scratch(nsub, rows, sub):
    half = nsub // 2 if nsub % 2 == 0 else nsub
    return {
        "map": pltpu.VMEM((nsub, sub, sub), F32),
        "mate_map": pltpu.VMEM((half, sub, sub), F32),
        "two": pltpu.VMEM((half, sub, sub), F32),
        "join_h": pltpu.VMEM((half, sub, 2 * sub), BF16),
        "join_l": pltpu.VMEM((half, sub, 2 * sub), BF16),
        "mate_off": pltpu.VMEM((half, rows, sub), F32),
        "join_off": pltpu.VMEM((half, rows, 2 * sub), F32),
        "arrived": pltpu.VMEM((half, rows, sub), F32),
        "out": pltpu.VMEM((half, rows, sub), F32),
        "hand": pltpu.VMEM((half, rows, sub), F32),
        "into": pltpu.VMEM((nsub, rows, sub), F32),
        "sem": pltpu.SemaphoreType.DMA((2, 2 + 2 * half)),
    }


def on_device(n_tm, n_sp, sections, right_side, tip_side, diag_inverse, fwd, bwd, arrow_rows, tip_inverse):
    T, rows, total_width = right_side.shape
    width, sub = fwd.shape[1], fwd.shape[2]
    nsub = width // sub
    F = arrow_rows.shape[1]
    both = rows + F
    vmem = pl.BlockSpec(memory_space=pltpu.VMEM)
    maps = pltpu.VMEM((nsub, sub, T * sub), BF16)
    dma = pltpu.SemaphoreType.DMA
    others = n_sp - 1
    states, turned = pl.pallas_call(
        functools.partial(kernel, n_tm, n_sp),
        out_shape=(
            jax.ShapeDtypeStruct((T, rows, width), F32),
            jax.ShapeDtypeStruct(tip_side.shape[::-1], F32),
        ),
        in_specs=[
            pl.BlockSpec(memory_space=pltpu.SMEM),
            vmem,
            vmem,
            pl.BlockSpec(memory_space=pl.ANY),
            vmem,
            vmem,
            vmem,
            vmem,
        ],
        out_specs=(vmem, vmem),
        scratch_shapes=[
            pltpu.VMEM(diag_inverse.shape, BF16),
            maps,
            maps,
            maps,
            maps,
            pltpu.VMEM((T, nsub, rows, sub), F32),
            pltpu.VMEM((T, 2 * rows, width), BF16),
            pltpu.VMEM((T, nsub, both, sub), F32),
            pltpu.VMEM((others, T, nsub, rows, sub), F32),
            pltpu.VMEM((others, T, nsub, rows, sub), F32),
            pltpu.VMEM((T, nsub, rows, sub), F32),
            pltpu.VMEM((others, T, nsub, F, sub), F32),
            pltpu.VMEM((others, T, nsub, F, sub), F32),
            pltpu.VMEM((F, 2 * rows), F32),
            pltpu.VMEM((n_sp, F, 2 * rows), F32),
            pltpu.VMEM((n_tm, F, 2 * rows), F32),
            pltpu.VMEM((F, 2 * rows), F32),
            scan_scratch(nsub, rows, sub),
            scan_scratch(nsub, both, sub),
            dma((T,)),
            dma((others, T, 2)),
            dma((others, T, 2)),
            dma((T, 2)),
            dma((T,)),
            dma((others,)),
            dma((others,)),
            dma((others,)),
            dma((n_sp,)),
            dma((n_tm - 1,)),
            dma((n_tm,)),
        ],
        compiler_params=pltpu.CompilerParams(
            collective_id=0, has_side_effects=True, vmem_limit_bytes=56 * 1024 * 1024
        ),
        cost_estimate=pl.CostEstimate(
            flops=8 * T * rows * width * total_width, bytes_accessed=2 * diag_inverse.size, transcendentals=0
        ),
    )(sections, right_side, tip_side.T, diag_inverse, fwd, bwd, arrow_rows, tip_inverse)
    return states, turned.T


def solution(mesh):
    placed = (
        P(),
        P("tm", None, None),
        P(),
        P("tm", "space", None),
        P("tm", "space", None),
        P("tm", "space", None),
        P("tm", None, "space"),
        P(),
    )
    return jax.shard_map(
        functools.partial(on_device, mesh.shape["tm"], mesh.shape["space"]),
        mesh=mesh,
        in_specs=placed,
        out_specs=(P("tm", None, "space"), P()),
        check_vma=False,
    )
```

time: 71.4 us -> 62.9 us (0.88)
  Pallas kernels: 65.8 us -> 58.1 us
  local copies, waits for them, and re-layouts: 4.67 us -> 3.13 us
    pallas_call x1, Pallas kernels: 65.8 us -> 58.1 us  [on_device(): pl.pallas_call(functools.partial(kernel, n_tm, n_sp), out_shape=(jax.Shap...]
    pallas_call x1 -> x0, local copies, waits for them, and re-layouts: 1.42 us -> none  [on_device(): pl.pallas_call(functools.partial(kernel, n_tm, n_sp), out_shape=(jax.Shap...]
where the time goes in v2:
time: 62.9 us; the launch traced here: 61.9 us
  Pallas kernels  58.1 us (92%)
  local copies, waits for them, and re-layouts  3.13 us (5%)
  between operations  0.64 us (1%)
    pallas_call x1, Pallas kernels, on_device(): pl.pallas_call(functools.partial(kernel, n_tm, n_sp), out_shape=(jax.Shap...  58.1 us
    unnamed x2, local copies, waits for them, and re-layouts  3.13 us

profile of v2, /device:TPU:0, one launch (start us, length us, event | category | flops | bytes accessed | tf_op | source)
XLA Modules:
  0.0 61.9 jit_solution(9650867590776619097)
XLA Ops:
  0.6 58.1 %shard_map.95 = (f32[4,64,512]{2,1,0:T(8,128)}, f32[8,64]{1,0:T(8,128)}) custom-call(s32[8]{0:T(128)} %sec.1, bf16[4,64,2048]{2,1,0:T(8,128)(2,1)} %rs.1, f32[8,64]{1,0:T(8,128)} %bitcast.2, bf16[4,512,2048]{2,1,0:T(8,128)(2,1)} %diag_hbm.1, bf16[4,512,128]{2,1,0:T(8,128)(2,1)} %fc.1, bf16[4,512,128]{2,1,0:T(8,128)(2,1)} %bc.1, bf16[4,8,512]{2,1,0:T(8,128)(2,1)} %arrow.1, ...), custom_call_target="tpu_custom_call" | custom-call | flops 2147483648 | bytes 8388608 | tf_op jit(solution)/shard_map/pallas_call | solution.py:458
  58.8 1.9 %copy.12 = f32[4,64,512]{2,1,0:T(8,128)} copy(f32[4,64,512]{2,1,0:T(8,128)} %get-tuple-element.8) | data formatting | bytes 1048576
  60.6 1.3 %copy.13 = f32[64,8]{0,1:T(8,128)} copy(f32[64,8]{0,1:T(8,128)} %bitcast.3) | data formatting | bytes 4096

commit v3 on v2

--- a/solution.py
+++ b/solution.py
@@ -40,7 +40,7 @@
     n_tm, n_sp, sec, rs, tip_side, diag_hbm, fc, bc, arrow, tip_inv,
     sol, tip_out,
     diag, fmap_h, fmap_l, bmap_h, bmap_l, driven, f_split, g_loc,
-    w_send, w_recv, w_pass, v_send, v_recv, part, gath_sp, gath_tm, mine_tm,
+    w_send, w_recv, w_pass, v_send, v_recv, v_own, part, gath_sp, gath_tm, mine_tm,
     f_scan, b_scan,
     diag_sem, ws_sem, wr_sem, ps_sem, pr_sem, vs_sem, vr_sem, as_sem, ar_sem, ts_sem, tr_sem,
 ):
@@ -81,19 +81,22 @@
             src_ref=src, dst_ref=dst, send_sem=send, recv_sem=recv, device_id=to, device_id_type=MESH
         )
 
-    def section_maps(coupling, order, high_ref, low_ref, own_map):
+    def section_maps(jobs):
         row = lax.broadcasted_iota(jnp.int32, (sub, sub), 0)
         col = lax.broadcasted_iota(jnp.int32, (sub, sub), 1)
         eye = jnp.where(row == col, 1.0, 0.0).astype(F32)
-        maps = [eye] * nsub
-        for t in order:
+        maps = [[eye] * nsub for _ in jobs]
+        for i in range(T):
+            for own, (coupling, order, high_ref, low_ref, _) in zip(maps, jobs):
+                t = order[i]
+                for n in range(nsub):
+                    own[n] = select(t, -couple(own[n], coupling[t, cols(n), :]), own[n])
+                    high = own[n].astype(BF16)
+                    high_ref[n, :, cols(t)] = high
+                    low_ref[n, :, cols(t)] = (own[n] - high.astype(F32)).astype(BF16)
+        for own, job in zip(maps, jobs):
             for n in range(nsub):
-                maps[n] = select(t, -couple(maps[n], coupling[t, cols(n), :]), maps[n])
-                high = maps[n].astype(BF16)
-                high_ref[n, :, cols(t)] = high
-                low_ref[n, :, cols(t)] = (maps[n] - high.astype(F32)).astype(BF16)
-        for n in range(nsub):
-            own_map[n] = maps[n]
+                job[4][n] = own[n]
 
     def in_order(mine, theirs, lead):
         ahead = jnp.full(mine.shape, core, jnp.int32) == lead
@@ -145,21 +148,34 @@
         )
 
     def chain(scan, first, last, to, lead):
+        def give(j, value):
+            scan["out"][j] = value
+            hop_copy(scan, j, to).start()
+
         @pl.when(first)
         def _():
             scan["arrived"][...] = jnp.zeros(scan["arrived"].shape, F32)
+            for j in range(half):
+                give(j, scan["join_off"][j, :, cols(0)])
+
+        @pl.when(jnp.logical_not(first))
+        def _():
+            for j in range(half):
+                hop_copy(scan, j, to).wait_recv()
+
+                @pl.when(jnp.logical_not(last))
+                def _():
+                    after = apply_map(scan["arrived"][j], scan["join_h"][j, :, cols(0)], scan["join_l"][j, :, cols(0)])
+                    give(j, scan["join_off"][j, :, cols(0)] + after)
 
         for j in range(half):
-            pl.when(jnp.logical_not(first))(hop_copy(scan, j, to).wait_recv)
             arrived = scan["arrived"][j]
-            after = scan["join_off"][j] + apply_map(arrived, scan["join_h"][j], scan["join_l"][j])
-            scan["out"][j] = after[:, :sub]
-            pl.when(jnp.logical_not(last))(hop_copy(scan, j, to).start)
-            mine, theirs = in_order(arrived, after[:, sub:], lead)
-            scan["into"][base + j] = mine
+            after = apply_map(arrived, scan["join_h"][j, :, cols(1)], scan["join_l"][j, :, cols(1)])
+            mine, theirs = in_order(arrived, scan["join_off"][j, :, cols(1)] + after, lead)
             if split:
                 scan["hand"][j] = theirs
                 hand_copy(scan, j, base).start()
+            scan["into"][base + j] = mine
         if split:
             for j in range(half):
                 hand_copy(scan, j, other_base).wait_recv()
@@ -175,9 +191,8 @@
     f_first, f_last, f_to = chip == 0, chip == chips - 1, lax.rem(s + 2, n_tm)
     b_first, b_last, b_to = f_last, f_first, lax.rem(s + n_tm - 2, n_tm)
 
-    section_maps(fc, range(T), fmap_h, fmap_l, f_scan["map"])
-    pl.semaphore_wait(barrier, n_tm - 1 + n_sp - 1)
-    map_copy(f_scan).start()
+    up, down = list(range(T)), list(range(T - 1, -1, -1))
+    section_maps(((fc, up, fmap_h, fmap_l, f_scan["map"]), (bc, down, bmap_h, bmap_l, b_scan["map"])))
     carry = [None] * nsub
     for t in range(T):
         loads[t].wait()
@@ -188,13 +203,14 @@
                 new = select(t, new - couple(carry[n], fc[t, cols(n), :]), carry[n])
             carry[n] = new
             driven[t, n] = new
+    pl.semaphore_wait(barrier, n_tm - 1 + n_sp - 1)
+    map_copy(f_scan).start()
     off_copy(f_scan, driven.at[T - 1]).start()
+    map_copy(b_scan).start()
     join_maps(f_scan, 0)
     join_offsets(f_scan, driven.at[T - 1], 0)
 
     def early():
-        section_maps(bc, range(T - 1, -1, -1), bmap_h, bmap_l, b_scan["map"])
-        map_copy(b_scan).start()
         for q in range(n_sp - 1):
 
             @pl.when(p > q)
@@ -209,14 +225,6 @@
 
     chain(f_scan, f_first, f_last, f_to, 0)
 
-    for n in range(nsub):
-        states = apply_map(f_scan["into"][n], fmap_h[n], fmap_l[n])
-        for t in range(T):
-            state = driven[t, n] + states[:, cols(t)]
-            state = select(t, state, jnp.zeros_like(state))
-            f_split[t, :, cols(n)] = stacked(state)
-
-    down = range(T - 1, -1, -1)
     merging = n_sp == 4 and nsub % 2 == 0
     mid = nsub // 2
 
@@ -246,14 +254,44 @@
         for n in range(nsub) if h is None else range(h * mid, h * mid + mid):
             w_send[q, t, n] += w_pass[t, n]
 
-    if merging:
-
-        @pl.when(p == 3)
-        def _():
-            for t in down:
+    for t in down:
+        for n in range(nsub):
+            state = driven[t, n] + apply_map(f_scan["into"][n], fmap_h[n, :, cols(t)], fmap_l[n, :, cols(t)])
+            state = select(t, state, jnp.zeros_like(state))
+            f_split[t, :, cols(n)] = stacked(state)
+
+        if merging:
+
+            @pl.when(p == 3)
+            def _():
                 product(0, t)
                 passing(0, t, 2, 0).start()
                 passing(0, t, 1, 1).start()
+
+            @pl.when(p == 2)
+            def _():
+                product(1, t)
+                passing(1, t, 3, None).start()
+                product(0, t)
+                final(0, t, 1, 1).start()
+
+            @pl.when(p == 1)
+            def _():
+                product(0, t)
+                final(0, t, 0, 0).start()
+
+        else:
+            for q in range(n_sp - 1):
+
+                @pl.when(p > q)
+                def _():
+                    product(q, t)
+                    final(q, t, p - 1, None).start()
+
+    if merging:
+
+        @pl.when(p == 3)
+        def _():
             for t in down:
                 product(2, t)
                 final(2, t, 0, None).start()
@@ -264,31 +302,14 @@
         @pl.when(p == 2)
         def _():
             for t in down:
-                product(1, t)
-                passing(1, t, 3, None).start()
-                product(0, t)
-                final(0, t, 1, 1).start()
-            for t in down:
                 merge(0, t, 0)
                 final(0, t, 1, 0).start()
 
         @pl.when(p == 1)
         def _():
-            for t in down:
-                product(0, t)
-                final(0, t, 0, 0).start()
             for t in down:
                 merge(0, t, 1)
                 final(0, t, 0, 1).start()
-
-    else:
-        for q in range(n_sp - 1):
-
-            @pl.when(p > q)
-            def _():
-                for t in down:
-                    product(q, t)
-                    final(q, t, p - 1, None).start()
 
     total = jnp.zeros((F, 2 * rows), F32)
     for t in range(T):
@@ -307,8 +328,8 @@
         full = folded(dot(f_split[t], block, ((1,), (0,))))
         arrow_full = dot(arrow[t], block, ((1,), (0,)))
         for n in range(nsub):
-            g_loc[t, n, :rows] = full[:, cols(n)]
-            g_loc[t, n, rows:] = arrow_full[:, cols(n)]
+            g_loc[t, n] = full[:, cols(n)]
+            v_own[t, n] = arrow_full[:, cols(n)]
 
     for d in range(1, n_sp):
         come = lax.rem(p + d, n_sp)
@@ -328,42 +349,7 @@
             remote(v_send.at[0], v_recv.at[q - 1], vs_sem.at[0], vr_sem.at[q - 1], {"space": q}).wait_recv()
             for t in range(T):
                 for n in range(nsub):
-                    g_loc[t, n, rows:] += v_recv[q - 1, t, n]
-
-    def take(t, slot, parts):
-        for h in parts:
-            final(0, t, slot, h).wait_recv()
-        for n in range(nsub):
-            g_loc[t, n, :rows] += w_recv[slot, t, n]
-
-    for t in down:
-        if merging:
-
-            @pl.when(p == 0)
-            def _():
-                take(t, 0, (0, 1))
-                take(t, 1, (0, 1))
-
-            @pl.when(jnp.logical_or(p == 1, p == 2))
-            def _():
-                take(t, 0, (None,))
-
-        else:
-            for q in range(1, n_sp):
-                pl.when(p < q)(functools.partial(take, t, q - 1, (None,)))
-
-        for n in range(nsub):
-            new = g_loc[t, n]
-            if t < T - 1:
-                old = g_loc[t + 1, n]
-                new = select(t, new - couple(old, bc[t, cols(n), :]), old)
-            else:
-                new = select(t, new, jnp.zeros_like(new))
-            g_loc[t, n] = new
-
-    off_copy(b_scan, g_loc.at[0]).start()
-    join_offsets(b_scan, g_loc.at[0], 1)
-    chain(b_scan, b_first, b_last, b_to, 1)
+                    v_own[t, n] += v_recv[q - 1, t, n]
 
     for d in range(1, n_tm):
         come = lax.rem(s + d, n_tm)
@@ -380,12 +366,49 @@
     tip_out[...] = turned
     tip = turned.T
 
+    for t in range(T):
+        for n in range(nsub):
+            g_loc[t, n] -= exact(tip, v_own[t, n], (((1,), (0,)), ((), ())))
+
+    def take(t, slot, parts):
+        for h in parts:
+            final(0, t, slot, h).wait_recv()
+        for n in range(nsub):
+            g_loc[t, n] += w_recv[slot, t, n]
+
+    for t in down:
+        if merging:
+
+            @pl.when(p == 0)
+            def _():
+                take(t, 0, (0, 1))
+                take(t, 1, (0, 1))
+
+            @pl.when(jnp.logical_or(p == 1, p == 2))
+            def _():
+                take(t, 0, (None,))
+
+        else:
+            for q in range(1, n_sp):
+                pl.when(p < q)(functools.partial(take, t, q - 1, (None,)))
+
+        for n in range(nsub):
+            new = g_loc[t, n]
+            if t < T - 1:
+                old = g_loc[t + 1, n]
+                new = select(t, new - couple(old, bc[t, cols(n), :]), old)
+            else:
+                new = select(t, new, jnp.zeros_like(new))
+            g_loc[t, n] = new
+
+    off_copy(b_scan, g_loc.at[0]).start()
+    join_offsets(b_scan, g_loc.at[0], 1)
+    chain(b_scan, b_first, b_last, b_to, 1)
+
     for n in range(nsub):
         states = apply_map(b_scan["into"][n], bmap_h[n], bmap_l[n])
         for t in range(T):
-            state = g_loc[t, n] + states[:, cols(t)]
-            value = state[:rows] - exact(tip, state[rows:], (((1,), (0,)), ((), ())))
-            sol[t, :, cols(n)] = select(t, value, jnp.zeros_like(value))
+            sol[t, :, cols(n)] = g_loc[t, n] + states[:, cols(t)]
 
     scan_end(f_scan, driven.at[T - 1], f_last, f_to)
     scan_end(b_scan, g_loc.at[0], b_last, b_to)
@@ -425,6 +448,14 @@
         remote(part, gath_sp.at[p], as_sem.at[d - 1], ar_sem.at[p], {"space": lax.rem(p + d, n_sp)}).wait_send()
     for d in range(1, n_tm):
         remote(mine_tm, gath_tm.at[s], ts_sem.at[d - 1], tr_sem.at[s], {"tm": lax.rem(s + d, n_tm)}).wait_send()
+
+
+def finish(sec, states, turned, sol, tip):
+    length = sec[lax.axis_index("tm")]
+    for t in range(states.shape[0]):
+        live = jnp.full(states.shape[1:], length, jnp.int32) > t
+        sol[t] = jnp.where(live, states[t], jnp.zeros_like(states[t]))
+    tip[...] = turned[...]
 
 
 def scan_scratch(nsub, rows, sub):
@@ -450,7 +481,6 @@
     width, sub = fwd.shape[1], fwd.shape[2]
     nsub = width // sub
     F = arrow_rows.shape[1]
-    both = rows + F
     vmem = pl.BlockSpec(memory_space=pltpu.VMEM)
     maps = pltpu.VMEM((nsub, sub, T * sub), BF16)
     dma = pltpu.SemaphoreType.DMA
@@ -480,18 +510,19 @@
             maps,
             pltpu.VMEM((T, nsub, rows, sub), F32),
             pltpu.VMEM((T, 2 * rows, width), BF16),
-            pltpu.VMEM((T, nsub, both, sub), F32),
+            pltpu.VMEM((T, nsub, rows, sub), F32),
             pltpu.VMEM((others, T, nsub, rows, sub), F32),
             pltpu.VMEM((others, T, nsub, rows, sub), F32),
             pltpu.VMEM((T, nsub, rows, sub), F32),
             pltpu.VMEM((others, T, nsub, F, sub), F32),
             pltpu.VMEM((others, T, nsub, F, sub), F32),
+            pltpu.VMEM((T, nsub, F, sub), F32),
             pltpu.VMEM((F, 2 * rows), F32),
             pltpu.VMEM((n_sp, F, 2 * rows), F32),
             pltpu.VMEM((n_tm, F, 2 * rows), F32),
             pltpu.VMEM((F, 2 * rows), F32),
             scan_scratch(nsub, rows, sub),
-            scan_scratch(nsub, both, sub),
+            scan_scratch(nsub, rows, sub),
             dma((T,)),
             dma((others, T, 2)),
             dma((others, T, 2)),
@@ -511,6 +542,15 @@
             flops=8 * T * rows * width * total_width, bytes_accessed=2 * diag_inverse.size, transcendentals=0
         ),
     )(sections, right_side, tip_side.T, diag_inverse, fwd, bwd, arrow_rows, tip_inverse)
+    states, turned = pl.pallas_call(
+        finish,
+        out_shape=(
+            jax.ShapeDtypeStruct(states.shape, F32),
+            jax.ShapeDtypeStruct(turned.shape, F32),
+        ),
+        in_specs=[pl.BlockSpec(memory_space=pltpu.SMEM), vmem, vmem],
+        out_specs=(vmem, vmem),
+    )(sections, states, turned)
     return states, turned.T
 
 

time: 62.9 us -> 59.8 us (0.951)
  local copies, waits for them, and re-layouts: 3.13 us -> 0 us
    unnamed x2 -> x0, local copies, waits for them, and re-layouts: 3.13 us -> none
    pallas_call x0 -> x1, Pallas kernels: none -> 1.9 us  [on_device(): pl.pallas_call(finish, out_shape=(jax.ShapeDtypeStruct(states.shape, F32)...]
    pallas_call x1, Pallas kernels: 58.1 us -> 56.7 us  [on_device(): pl.pallas_call(functools.partial(kernel, n_tm, n_sp), out_shape=(jax.Shap...]
where the time goes in v3:
time: 59.8 us; the launch traced here: 59.3 us
  Pallas kernels  58.6 us (98%)
  between operations  0.64 us (1%)
    pallas_call x1, Pallas kernels, on_device(): pl.pallas_call(functools.partial(kernel, n_tm, n_sp), out_shape=(jax.Shap...  56.7 us
    pallas_call x1, Pallas kernels, on_device(): pl.pallas_call(finish, out_shape=(jax.ShapeDtypeStruct(states.shape, F32)...  1.9 us

profile of v3, /device:TPU:0, one launch (start us, length us, event | category | flops | bytes accessed | tf_op | source)
XLA Modules:
  0.0 59.3 jit_solution(14359352277091742800)
XLA Ops:
  0.6 56.7 %shard_map.95 = (f32[4,64,512]{2,1,0:T(8,128)}, f32[8,64]{1,0:T(8,128)}) custom-call(s32[8]{0:T(128)} %sec.3, bf16[4,64,2048]{2,1,0:T(8,128)(2,1)} %rs.1, f32[8,64]{1,0:T(8,128)} %bitcast.2, bf16[4,512,2048]{2,1,0:T(8,128)(2,1)} %diag_hbm.1, bf16[4,512,128]{2,1,0:T(8,128)(2,1)} %fc.1, bf16[4,512,128]{2,1,0:T(8,128)(2,1)} %bc.1, bf16[4,8,512]{2,1,0:T(8,128)(2,1)} %arrow.1, ...), custom_call_target="tpu_custom_call" | custom-call | flops 2147483648 | bytes 8388608 | tf_op jit(solution)/shard_map/pallas_call | solution.py:488
  57.4 1.9 %shard_map.96 = (f32[4,64,512]{2,1,0:T(8,128)}, f32[8,64]{1,0:T(8,128)}) custom-call(s32[8]{0:T(128)} %sec.3, f32[4,64,512]{2,1,0:T(8,128)} %get-tuple-element.6.states, f32[8,64]{1,0:T(8,128)} %get-tuple-element.7.turned), custom_call_target="tpu_custom_call" | custom-call | tf_op jit(solution)/shard_map/pallas_call | solution.py:545

commit v4 on v3

--- a/solution.py
+++ b/solution.py
@@ -30,22 +30,34 @@
     return folded(dot(stacked(x), block, ((1,), (1,))))
 
 
+def halves(x):
+    high = x.astype(BF16)
+    return high, (x - high.astype(F32)).astype(BF16)
+
+
 def apply_map(x, high, low):
     rows = x.shape[0]
     pieces = stacked(x)
+    return folded(dot(pieces, high, ((1,), (1,)))) + dot(pieces[:rows], low, ((1,), (1,)))
+
+
+def product_of(x, y):
+    high, low = halves(y)
+    rows = x.shape[0]
+    pieces = stacked(x)
     return folded(dot(pieces, high, ((1,), (0,)))) + dot(pieces[:rows], low, ((1,), (0,)))
 
 
 def kernel(
-    n_tm, n_sp, sec, rs, tip_side, diag_hbm, fc, bc, arrow, tip_inv,
+    n_tm, n_sp, sec, rs_hbm, tip_side, diag_hbm, fc_hbm, bc_hbm, arrow, tip_inv,
     sol, tip_out,
-    diag, fmap_h, fmap_l, bmap_h, bmap_l, driven, f_split, g_loc,
+    rs, fc, bc, diag, fmap_h, fmap_l, bmap_h, bmap_l, driven, f_split, g_loc,
     w_send, w_recv, w_pass, v_send, v_recv, v_own, part, gath_sp, gath_tm, mine_tm,
     f_scan, b_scan,
-    diag_sem, ws_sem, wr_sem, ps_sem, pr_sem, vs_sem, vr_sem, as_sem, ar_sem, ts_sem, tr_sem,
+    in_sem, diag_sem, ws_sem, wr_sem, ps_sem, pr_sem, vs_sem, vr_sem, as_sem, ar_sem, ts_sem, tr_sem,
 ):
-    T, rows = rs.shape[0], rs.shape[1]
-    width, sub = fc.shape[1], fc.shape[2]
+    T, rows = rs_hbm.shape[0], rs_hbm.shape[1]
+    width, sub = fc_hbm.shape[1], fc_hbm.shape[2]
     nsub = width // sub
     F = arrow.shape[1]
     s, p = lax.axis_index("tm"), lax.axis_index("space")
@@ -56,10 +68,14 @@
     other_base = half - core * half if split else 0
     mate = s + 1 - 2 * core
 
+    first_loads = [
+        pltpu.make_async_copy(src, dst, in_sem.at[i])
+        for i, (src, dst) in enumerate(((fc_hbm, fc), (rs_hbm, rs), (bc_hbm, bc)))
+    ]
     loads = [
         pltpu.make_async_copy(diag_hbm.at[t], diag.at[t], diag_sem.at[t]) for t in range(T)
     ]
-    for load in loads:
+    for load in first_loads[:2] + loads + first_loads[2:]:
         load.start()
 
     barrier = pltpu.get_barrier_semaphore()
@@ -81,22 +97,22 @@
             src_ref=src, dst_ref=dst, send_sem=send, recv_sem=recv, device_id=to, device_id_type=MESH
         )
 
-    def section_maps(jobs):
+    def section_maps(coupling, order, high_ref, low_ref, own_map):
         row = lax.broadcasted_iota(jnp.int32, (sub, sub), 0)
         col = lax.broadcasted_iota(jnp.int32, (sub, sub), 1)
-        eye = jnp.where(row == col, 1.0, 0.0).astype(F32)
-        maps = [[eye] * nsub for _ in jobs]
-        for i in range(T):
-            for own, (coupling, order, high_ref, low_ref, _) in zip(maps, jobs):
-                t = order[i]
-                for n in range(nsub):
-                    own[n] = select(t, -couple(own[n], coupling[t, cols(n), :]), own[n])
-                    high = own[n].astype(BF16)
-                    high_ref[n, :, cols(t)] = high
-                    low_ref[n, :, cols(t)] = (own[n] - high.astype(F32)).astype(BF16)
-        for own, job in zip(maps, jobs):
+        maps = [jnp.where(row == col, 1.0, 0.0).astype(F32)] * nsub
+        for i, t in enumerate(order):
             for n in range(nsub):
-                job[4][n] = own[n]
+                block = coupling[t, cols(n), :]
+                if i == 0:
+                    new = -block.astype(F32)
+                else:
+                    both = dot(block, jnp.concatenate(halves(maps[n]), 1), ((1,), (0,)))
+                    new = -(both[:, :sub] + both[:, sub:])
+                maps[n] = select(t, new, maps[n])
+                high_ref[n, cols(t), :], low_ref[n, cols(t), :] = halves(maps[n])
+        for n in range(nsub):
+            own_map[n] = maps[n]
 
     def in_order(mine, theirs, lead):
         ahead = jnp.full(mine.shape, core, jnp.int32) == lead
@@ -115,24 +131,17 @@
         )
 
     def join_maps(scan, lead):
-        map_copy(scan).wait_recv()
         for j in range(half):
             one, two = in_order(scan["map"][base + j], scan["mate_map"][j], lead)
-            high = two.astype(BF16)
-            both = apply_map(one, high, (two - high.astype(F32)).astype(BF16))
-            for i, value in enumerate((both, one)):
-                high = value.astype(BF16)
-                scan["join_h"][j, :, cols(i)] = high
-                scan["join_l"][j, :, cols(i)] = (value - high.astype(F32)).astype(BF16)
-            scan["two"][j] = two
+            for i, value in enumerate((product_of(two, one), one)):
+                scan["join_h"][j, cols(i), :], scan["join_l"][j, cols(i), :] = halves(value)
 
     def join_offsets(scan, own, lead):
         off_copy(scan, own).wait_recv()
         for j in range(half):
+            _, after = in_order(scan["map"][base + j], scan["mate_map"][j], lead)
             one, two = in_order(own[base + j], scan["mate_off"][j], lead)
-            after = scan["two"][j]
-            high = after.astype(BF16)
-            scan["join_off"][j, :, cols(0)] = two + apply_map(one, high, (after - high.astype(F32)).astype(BF16))
+            scan["join_off"][j, :, cols(0)] = two + apply_map(one, *halves(after))
             scan["join_off"][j, :, cols(1)] = one
 
     def hop_copy(scan, j, to):
@@ -147,17 +156,18 @@
             scan["sem"].at[0, 2 + half + j], scan["sem"].at[1, 2 + half + j], {"tm": mate},
         )
 
-    def chain(scan, first, last, to, lead):
-        def give(j, value):
-            scan["out"][j] = value
-            hop_copy(scan, j, to).start()
-
+    def give(scan, j, to, value):
+        scan["out"][j] = value
+        hop_copy(scan, j, to).start()
+
+    def chain_start(scan, first, to):
         @pl.when(first)
         def _():
             scan["arrived"][...] = jnp.zeros(scan["arrived"].shape, F32)
             for j in range(half):
-                give(j, scan["join_off"][j, :, cols(0)])
-
+                give(scan, j, to, scan["join_off"][j, :, cols(0)])
+
+    def chain(scan, first, last, to, lead):
         @pl.when(jnp.logical_not(first))
         def _():
             for j in range(half):
@@ -165,20 +175,20 @@
 
                 @pl.when(jnp.logical_not(last))
                 def _():
-                    after = apply_map(scan["arrived"][j], scan["join_h"][j, :, cols(0)], scan["join_l"][j, :, cols(0)])
-                    give(j, scan["join_off"][j, :, cols(0)] + after)
+                    after = apply_map(scan["arrived"][j], scan["join_h"][j, cols(0), :], scan["join_l"][j, cols(0), :])
+                    give(scan, j, to, scan["join_off"][j, :, cols(0)] + after)
 
         for j in range(half):
             arrived = scan["arrived"][j]
-            after = apply_map(arrived, scan["join_h"][j, :, cols(1)], scan["join_l"][j, :, cols(1)])
+            after = apply_map(arrived, scan["join_h"][j, cols(1), :], scan["join_l"][j, cols(1), :])
             mine, theirs = in_order(arrived, scan["join_off"][j, :, cols(1)] + after, lead)
             if split:
                 scan["hand"][j] = theirs
                 hand_copy(scan, j, base).start()
             scan["into"][base + j] = mine
-        if split:
-            for j in range(half):
-                hand_copy(scan, j, other_base).wait_recv()
+
+    def lanes(n):
+        return pl.ds(pl.multiple_of(n * sub, sub), sub)
 
     def scan_end(scan, own, last, to):
         map_copy(scan).wait_send()
@@ -192,7 +202,9 @@
     b_first, b_last, b_to = f_last, f_first, lax.rem(s + n_tm - 2, n_tm)
 
     up, down = list(range(T)), list(range(T - 1, -1, -1))
-    section_maps(((fc, up, fmap_h, fmap_l, f_scan["map"]), (bc, down, bmap_h, bmap_l, b_scan["map"])))
+    first_loads[0].wait()
+    section_maps(fc, up, fmap_h, fmap_l, f_scan["map"])
+    first_loads[1].wait()
     carry = [None] * nsub
     for t in range(T):
         loads[t].wait()
@@ -206,9 +218,14 @@
     pl.semaphore_wait(barrier, n_tm - 1 + n_sp - 1)
     map_copy(f_scan).start()
     off_copy(f_scan, driven.at[T - 1]).start()
+    for load in first_loads[2:]:
+        load.wait()
+    section_maps(bc, down, bmap_h, bmap_l, b_scan["map"])
     map_copy(b_scan).start()
+    map_copy(f_scan).wait_recv()
+    join_offsets(f_scan, driven.at[T - 1], 0)
+    chain_start(f_scan, f_first, f_to)
     join_maps(f_scan, 0)
-    join_offsets(f_scan, driven.at[T - 1], 0)
 
     def early():
         for q in range(n_sp - 1):
@@ -225,6 +242,18 @@
 
     chain(f_scan, f_first, f_last, f_to, 0)
 
+    def forward_state(t, n):
+        state = driven[t, n] + apply_map(f_scan["into"][n], fmap_h[n, cols(t), :], fmap_l[n, cols(t), :])
+        state = select(t, state, jnp.zeros_like(state))
+        f_split[t, :, lanes(n)] = stacked(state)
+
+    if split:
+        for t in down:
+            for j in range(half):
+                forward_state(t, base + j)
+        for j in range(half):
+            hand_copy(f_scan, j, other_base).wait_recv()
+
     merging = n_sp == 4 and nsub % 2 == 0
     mid = nsub // 2
 
@@ -255,10 +284,8 @@
             w_send[q, t, n] += w_pass[t, n]
 
     for t in down:
-        for n in range(nsub):
-            state = driven[t, n] + apply_map(f_scan["into"][n], fmap_h[n, :, cols(t)], fmap_l[n, :, cols(t)])
-            state = select(t, state, jnp.zeros_like(state))
-            f_split[t, :, cols(n)] = stacked(state)
+        for j in range(half):
+            forward_state(t, other_base + j)
 
         if merging:
 
@@ -320,6 +347,7 @@
         remote(part, gath_sp.at[p], as_sem.at[d - 1], ar_sem.at[p], {"space": lax.rem(p + d, n_sp)}).start()
 
     pl.when(chip < chips // 2)(early)
+    map_copy(b_scan).wait_recv()
     join_maps(b_scan, 1)
 
     own_cols = pl.ds(pl.multiple_of(p * width, width), width)
@@ -403,12 +431,21 @@
 
     off_copy(b_scan, g_loc.at[0]).start()
     join_offsets(b_scan, g_loc.at[0], 1)
+    chain_start(b_scan, b_first, b_to)
     chain(b_scan, b_first, b_last, b_to, 1)
 
-    for n in range(nsub):
+    def backward_states(n):
         states = apply_map(b_scan["into"][n], bmap_h[n], bmap_l[n])
         for t in range(T):
-            sol[t, :, cols(n)] = g_loc[t, n] + states[:, cols(t)]
+            sol[t, :, lanes(n)] = g_loc[t, n] + states[:, cols(t)]
+
+    if split:
+        for j in range(half):
+            backward_states(base + j)
+        for j in range(half):
+            hand_copy(b_scan, j, other_base).wait_recv()
+    for j in range(half):
+        backward_states(other_base + j)
 
     scan_end(f_scan, driven.at[T - 1], f_last, f_to)
     scan_end(b_scan, g_loc.at[0], b_last, b_to)
@@ -463,9 +500,8 @@
     return {
         "map": pltpu.VMEM((nsub, sub, sub), F32),
         "mate_map": pltpu.VMEM((half, sub, sub), F32),
-        "two": pltpu.VMEM((half, sub, sub), F32),
-        "join_h": pltpu.VMEM((half, sub, 2 * sub), BF16),
-        "join_l": pltpu.VMEM((half, sub, 2 * sub), BF16),
+        "join_h": pltpu.VMEM((half, 2 * sub, sub), BF16),
+        "join_l": pltpu.VMEM((half, 2 * sub, sub), BF16),
         "mate_off": pltpu.VMEM((half, rows, sub), F32),
         "join_off": pltpu.VMEM((half, rows, 2 * sub), F32),
         "arrived": pltpu.VMEM((half, rows, sub), F32),
@@ -481,8 +517,8 @@
     width, sub = fwd.shape[1], fwd.shape[2]
     nsub = width // sub
     F = arrow_rows.shape[1]
-    vmem = pl.BlockSpec(memory_space=pltpu.VMEM)
-    maps = pltpu.VMEM((nsub, sub, T * sub), BF16)
+    vmem, hbm = pl.BlockSpec(memory_space=pltpu.VMEM), pl.BlockSpec(memory_space=pl.ANY)
+    maps = pltpu.VMEM((nsub, T * sub, sub), BF16)
     dma = pltpu.SemaphoreType.DMA
     others = n_sp - 1
     states, turned = pl.pallas_call(
@@ -493,16 +529,19 @@
         ),
         in_specs=[
             pl.BlockSpec(memory_space=pltpu.SMEM),
+            hbm,
             vmem,
-            vmem,
-            pl.BlockSpec(memory_space=pl.ANY),
-            vmem,
-            vmem,
+            hbm,
+            hbm,
+            hbm,
             vmem,
             vmem,
         ],
         out_specs=(vmem, vmem),
         scratch_shapes=[
+            pltpu.VMEM(right_side.shape, BF16),
+            pltpu.VMEM(fwd.shape, BF16),
+            pltpu.VMEM(bwd.shape, BF16),
             pltpu.VMEM(diag_inverse.shape, BF16),
             maps,
             maps,
@@ -523,6 +562,7 @@
             pltpu.VMEM((F, 2 * rows), F32),
             scan_scratch(nsub, rows, sub),
             scan_scratch(nsub, rows, sub),
+            dma((3,)),
             dma((T,)),
             dma((others, T, 2)),
             dma((others, T, 2)),

time: 59.8 us -> 60.9 us (1.018)
  Pallas kernels: 58.6 us -> 59.8 us
    pallas_call x1, Pallas kernels: 56.7 us -> 57.9 us  [on_device(): pl.pallas_call(functools.partial(kernel, n_tm, n_sp), out_shape=(jax.Shap...]
where the time goes in v4:
time: 60.9 us; the launch traced here: 60.4 us
  Pallas kernels  59.8 us (98%)
  between operations  0.64 us (1%)
    pallas_call x1, Pallas kernels, on_device(): pl.pallas_call(functools.partial(kernel, n_tm, n_sp), out_shape=(jax.Shap...  57.9 us
    pallas_call x1, Pallas kernels, on_device(): pl.pallas_call(finish, out_shape=(jax.ShapeDtypeStruct(states.shape, F32)...  1.9 us

profile of v4, /device:TPU:0, one launch (start us, length us, event | category | flops | bytes accessed | tf_op | source)
XLA Modules:
  0.0 60.4 jit_solution(12797680985297945357)
XLA Ops:
  0.6 57.9 %shard_map.95 = (f32[4,64,512]{2,1,0:T(8,128)}, f32[8,64]{1,0:T(8,128)}) custom-call(s32[8]{0:T(128)} %sec.3, bf16[4,64,2048]{2,1,0:T(8,128)(2,1)} %rs_hbm.1, f32[8,64]{1,0:T(8,128)} %bitcast.2, bf16[4,512,2048]{2,1,0:T(8,128)(2,1)} %diag_hbm.1, bf16[4,512,128]{2,1,0:T(8,128)(2,1)} %fc_hbm.1, bf16[4,512,128]{2,1,0:T(8,128)(2,1)} %bc_hbm.1, ...), custom_call_target="tpu_custom_call" | custom-call | flops 2147483648 | bytes 8388608 | tf_op jit(solution)/shard_map/pallas_call | solution.py:524
  58.5 1.9 %shard_map.96 = (f32[4,64,512]{2,1,0:T(8,128)}, f32[8,64]{1,0:T(8,128)}) custom-call(s32[8]{0:T(128)} %sec.3, f32[4,64,512]{2,1,0:T(8,128)} %get-tuple-element.6.states, f32[8,64]{1,0:T(8,128)} %get-tuple-element.7.turned), custom_call_target="tpu_custom_call" | custom-call | tf_op jit(solution)/shard_map/pallas_call | solution.py:585

commit v5 on v4

--- a/solution.py
+++ b/solution.py
@@ -70,12 +70,12 @@
 
     first_loads = [
         pltpu.make_async_copy(src, dst, in_sem.at[i])
-        for i, (src, dst) in enumerate(((fc_hbm, fc), (rs_hbm, rs), (bc_hbm, bc)))
+        for i, (src, dst) in enumerate(((fc_hbm, fc), (bc_hbm, bc), (rs_hbm, rs)))
     ]
     loads = [
         pltpu.make_async_copy(diag_hbm.at[t], diag.at[t], diag_sem.at[t]) for t in range(T)
     ]
-    for load in first_loads[:2] + loads + first_loads[2:]:
+    for load in first_loads + loads:
         load.start()
 
     barrier = pltpu.get_barrier_semaphore()
@@ -130,24 +130,45 @@
             scan["sem"].at[0, 1], scan["sem"].at[1, 1], {"tm": mate},
         )
 
-    def join_maps(scan, lead):
+    def pair_map_copy(scan, way):
+        return remote(
+            scan["chip_map"], scan["ahead_map"],
+            scan["sem"].at[0, 2 + 2 * half], scan["sem"].at[1, 2 + 2 * half], {"tm": away(way, 2)},
+        )
+
+    def pair_off_copy(scan, j, way):
+        at = 3 + 2 * half + j
+        return remote(
+            scan["chip_off"].at[j], scan["ahead_off"].at[j],
+            scan["sem"].at[0, at], scan["sem"].at[1, at], {"tm": away(way, 2)},
+        )
+
+    def away(way, steps):
+        return lax.rem(s + n_tm + way * steps, n_tm)
+
+    def join_maps(scan, lead, first_of_pair, way):
         for j in range(half):
             one, two = in_order(scan["map"][base + j], scan["mate_map"][j], lead)
-            for i, value in enumerate((product_of(two, one), one)):
-                scan["join_h"][j, cols(i), :], scan["join_l"][j, cols(i), :] = halves(value)
-
-    def join_offsets(scan, own, lead):
+            scan["one_h"][j], scan["one_l"][j] = halves(one)
+            both = product_of(two, one)
+            scan["chip_map"][j] = both
+            scan["chip_h"][j], scan["chip_l"][j] = halves(both)
+        pl.when(first_of_pair)(pair_map_copy(scan, way).start)
+
+    def join_offsets(scan, own, lead, first_of_pair, way):
         off_copy(scan, own).wait_recv()
         for j in range(half):
             _, after = in_order(scan["map"][base + j], scan["mate_map"][j], lead)
             one, two = in_order(own[base + j], scan["mate_off"][j], lead)
-            scan["join_off"][j, :, cols(0)] = two + apply_map(one, *halves(after))
-            scan["join_off"][j, :, cols(1)] = one
-
-    def hop_copy(scan, j, to):
+            scan["chip_off"][j] = two + apply_map(one, *halves(after))
+            scan["one_off"][j] = one
+            pl.when(first_of_pair)(pair_off_copy(scan, j, way).start)
+
+    def hop_copy(scan, j, to, far):
+        at = 3 + 3 * half + j if far else 2 + j
         return remote(
             scan["out"].at[j], scan["arrived"].at[j],
-            scan["sem"].at[0, 2 + j], scan["sem"].at[1, 2 + j], {"tm": to},
+            scan["sem"].at[0, at], scan["sem"].at[1, 2 + j], {"tm": to},
         )
 
     def hand_copy(scan, j, at):
@@ -156,55 +177,88 @@
             scan["sem"].at[0, 2 + half + j], scan["sem"].at[1, 2 + half + j], {"tm": mate},
         )
 
-    def give(scan, j, to, value):
-        scan["out"][j] = value
-        hop_copy(scan, j, to).start()
-
-    def chain_start(scan, first, to):
-        @pl.when(first)
-        def _():
-            scan["arrived"][...] = jnp.zeros(scan["arrived"].shape, F32)
-            for j in range(half):
-                give(scan, j, to, scan["join_off"][j, :, cols(0)])
-
-    def chain(scan, first, last, to, lead):
-        @pl.when(jnp.logical_not(first))
-        def _():
-            for j in range(half):
-                hop_copy(scan, j, to).wait_recv()
-
-                @pl.when(jnp.logical_not(last))
-                def _():
-                    after = apply_map(scan["arrived"][j], scan["join_h"][j, cols(0), :], scan["join_l"][j, cols(0), :])
-                    give(scan, j, to, scan["join_off"][j, :, cols(0)] + after)
-
-        for j in range(half):
-            arrived = scan["arrived"][j]
-            after = apply_map(arrived, scan["join_h"][j, cols(1), :], scan["join_l"][j, cols(1), :])
-            mine, theirs = in_order(arrived, scan["join_off"][j, :, cols(1)] + after, lead)
+    def chain(scan, first, last, lead, first_of_pair, way):
+        second = jnp.logical_not(first_of_pair)
+        later = jnp.logical_not(first)
+
+        @pl.when(jnp.logical_and(second, later))
+        def _():
+            pair_map_copy(scan, way).wait_recv()
+
+        for j in range(half):
+
+            @pl.when(second)
+            def _():
+                pair_off_copy(scan, j, way).wait_recv()
+                scan["chip_in"][j] = scan["ahead_off"][j]
+
+            @pl.when(jnp.logical_and(first_of_pair, first))
+            def _():
+                scan["chip_in"][j] = jnp.zeros((rows, sub), F32)
+
+            pl.when(later)(hop_copy(scan, j, mate, False).wait_recv)
+
+            @pl.when(jnp.logical_and(first_of_pair, later))
+            def _():
+                scan["chip_in"][j] = scan["arrived"][j]
+
+            @pl.when(jnp.logical_and(second, later))
+            def _():
+                scan["chip_in"][j] += apply_map(scan["arrived"][j], *halves(scan["ahead_map"][j]))
+
+            @pl.when(jnp.logical_and(second, jnp.logical_not(last)))
+            def _():
+                after = apply_map(scan["chip_in"][j], scan["chip_h"][j], scan["chip_l"][j])
+                scan["out"][j] = scan["chip_off"][j] + after
+                hop_copy(scan, j, away(way, 4), True).start()
+                hop_copy(scan, j, away(way, 2), False).start()
+
+        for j in range(half):
+            chip_in = scan["chip_in"][j]
+            after = apply_map(chip_in, scan["one_h"][j], scan["one_l"][j])
+            mine, theirs = in_order(chip_in, scan["one_off"][j] + after, lead)
             if split:
                 scan["hand"][j] = theirs
                 hand_copy(scan, j, base).start()
             scan["into"][base + j] = mine
 
+        @pl.when(jnp.logical_and(second, first))
+        def _():
+            pair_map_copy(scan, way).wait_recv()
+
     def lanes(n):
         return pl.ds(pl.multiple_of(n * sub, sub), sub)
 
-    def scan_end(scan, own, last, to):
+    def scan_end(scan, own, last, first_of_pair, way):
         map_copy(scan).wait_send()
         off_copy(scan, own).wait_send()
-        for j in range(half):
-            pl.when(jnp.logical_not(last))(hop_copy(scan, j, to).wait_send)
-            if split:
+
+        @pl.when(first_of_pair)
+        def _():
+            pair_map_copy(scan, way).wait_send()
+            for j in range(half):
+                pair_off_copy(scan, j, way).wait_send()
+
+        @pl.when(jnp.logical_not(jnp.logical_or(first_of_pair, last)))
+        def _():
+            for j in range(half):
+                hop_copy(scan, j, away(way, 4), True).wait_send()
+                hop_copy(scan, j, away(way, 2), False).wait_send()
+
+        if split:
+            for j in range(half):
                 hand_copy(scan, j, base).wait_send()
 
-    f_first, f_last, f_to = chip == 0, chip == chips - 1, lax.rem(s + 2, n_tm)
-    b_first, b_last, b_to = f_last, f_first, lax.rem(s + n_tm - 2, n_tm)
+    f_first, f_last = chip // 2 == 0, chip // 2 == chips // 2 - 1
+    b_first, b_last = f_last, f_first
+    f_lead, b_lead = lax.rem(chip, 2) == 0, lax.rem(chip, 2) == 1
 
     up, down = list(range(T)), list(range(T - 1, -1, -1))
     first_loads[0].wait()
     section_maps(fc, up, fmap_h, fmap_l, f_scan["map"])
     first_loads[1].wait()
+    section_maps(bc, down, bmap_h, bmap_l, b_scan["map"])
+    first_loads[2].wait()
     carry = [None] * nsub
     for t in range(T):
         loads[t].wait()
@@ -218,14 +272,10 @@
     pl.semaphore_wait(barrier, n_tm - 1 + n_sp - 1)
     map_copy(f_scan).start()
     off_copy(f_scan, driven.at[T - 1]).start()
-    for load in first_loads[2:]:
-        load.wait()
-    section_maps(bc, down, bmap_h, bmap_l, b_scan["map"])
     map_copy(b_scan).start()
     map_copy(f_scan).wait_recv()
-    join_offsets(f_scan, driven.at[T - 1], 0)
-    chain_start(f_scan, f_first, f_to)
-    join_maps(f_scan, 0)
+    join_offsets(f_scan, driven.at[T - 1], 0, f_lead, 1)
+    join_maps(f_scan, 0, f_lead, 1)
 
     def early():
         for q in range(n_sp - 1):
@@ -240,7 +290,7 @@
 
     pl.when(chip >= chips // 2)(early)
 
-    chain(f_scan, f_first, f_last, f_to, 0)
+    chain(f_scan, f_first, f_last, 0, f_lead, 1)
 
     def forward_state(t, n):
         state = driven[t, n] + apply_map(f_scan["into"][n], fmap_h[n, cols(t), :], fmap_l[n, cols(t), :])
@@ -348,7 +398,7 @@
 
     pl.when(chip < chips // 2)(early)
     map_copy(b_scan).wait_recv()
-    join_maps(b_scan, 1)
+    join_maps(b_scan, 1, b_lead, -1)
 
     own_cols = pl.ds(pl.multiple_of(p * width, width), width)
     for t in range(T):
@@ -430,9 +480,8 @@
             g_loc[t, n] = new
 
     off_copy(b_scan, g_loc.at[0]).start()
-    join_offsets(b_scan, g_loc.at[0], 1)
-    chain_start(b_scan, b_first, b_to)
-    chain(b_scan, b_first, b_last, b_to, 1)
+    join_offsets(b_scan, g_loc.at[0], 1, b_lead, -1)
+    chain(b_scan, b_first, b_last, 1, b_lead, -1)
 
     def backward_states(n):
         states = apply_map(b_scan["into"][n], bmap_h[n], bmap_l[n])
@@ -447,8 +496,8 @@
     for j in range(half):
         backward_states(other_base + j)
 
-    scan_end(f_scan, driven.at[T - 1], f_last, f_to)
-    scan_end(b_scan, g_loc.at[0], b_last, b_to)
+    scan_end(f_scan, driven.at[T - 1], f_last, f_lead, 1)
+    scan_end(b_scan, g_loc.at[0], b_last, b_lead, -1)
     for q in range(n_sp - 1):
 
         @pl.when(p > q)
@@ -500,15 +549,22 @@
     return {
         "map": pltpu.VMEM((nsub, sub, sub), F32),
         "mate_map": pltpu.VMEM((half, sub, sub), F32),
-        "join_h": pltpu.VMEM((half, 2 * sub, sub), BF16),
-        "join_l": pltpu.VMEM((half, 2 * sub, sub), BF16),
+        "chip_map": pltpu.VMEM((half, sub, sub), F32),
+        "chip_h": pltpu.VMEM((half, sub, sub), BF16),
+        "chip_l": pltpu.VMEM((half, sub, sub), BF16),
+        "one_h": pltpu.VMEM((half, sub, sub), BF16),
+        "one_l": pltpu.VMEM((half, sub, sub), BF16),
+        "ahead_map": pltpu.VMEM((half, sub, sub), F32),
         "mate_off": pltpu.VMEM((half, rows, sub), F32),
-        "join_off": pltpu.VMEM((half, rows, 2 * sub), F32),
+        "chip_off": pltpu.VMEM((half, rows, sub), F32),
+        "one_off": pltpu.VMEM((half, rows, sub), F32),
+        "ahead_off": pltpu.VMEM((half, rows, sub), F32),
+        "chip_in": pltpu.VMEM((half, rows, sub), F32),
         "arrived": pltpu.VMEM((half, rows, sub), F32),
         "out": pltpu.VMEM((half, rows, sub), F32),
         "hand": pltpu.VMEM((half, rows, sub), F32),
         "into": pltpu.VMEM((nsub, rows, sub), F32),
-        "sem": pltpu.SemaphoreType.DMA((2, 2 + 2 * half)),
+        "sem": pltpu.SemaphoreType.DMA((2, 3 + 4 * half)),
     }
 
 

time: 60.9 us -> 59.8 us (0.982)
  Pallas kernels: 59.8 us -> 58.7 us
    pallas_call x1, Pallas kernels: 57.9 us -> 56.8 us  [on_device(): pl.pallas_call(functools.partial(kernel, n_tm, n_sp), out_shape=(jax.Shap...]
where the time goes in v5:
time: 59.8 us; the launch traced here: 59.3 us
  Pallas kernels  58.7 us (98%)
  between operations  0.64 us (1%)
    pallas_call x1, Pallas kernels, on_device(): pl.pallas_call(functools.partial(kernel, n_tm, n_sp), out_shape=(jax.Shap...  56.8 us
    pallas_call x1, Pallas kernels, on_device(): pl.pallas_call(finish, out_shape=(jax.ShapeDtypeStruct(states.shape, F32)...  1.9 us

profile of v5, /device:TPU:0, one launch (start us, length us, event | category | flops | bytes accessed | tf_op | source)
XLA Modules:
  0.0 59.3 jit_solution(18293917667201894566)
XLA Ops:
  0.6 56.8 %shard_map.95 = (f32[4,64,512]{2,1,0:T(8,128)}, f32[8,64]{1,0:T(8,128)}) custom-call(s32[8]{0:T(128)} %sec.3, bf16[4,64,2048]{2,1,0:T(8,128)(2,1)} %rs_hbm.1, f32[8,64]{1,0:T(8,128)} %bitcast.2, bf16[4,512,2048]{2,1,0:T(8,128)(2,1)} %diag_hbm.1, bf16[4,512,128]{2,1,0:T(8,128)(2,1)} %fc_hbm.1, bf16[4,512,128]{2,1,0:T(8,128)(2,1)} %bc_hbm.1, ...), custom_call_target="tpu_custom_call" | custom-call | flops 2147483648 | bytes 8388608 | tf_op jit(solution)/shard_map/pallas_call | solution.py:580
  57.4 1.9 %shard_map.96 = (f32[4,64,512]{2,1,0:T(8,128)}, f32[8,64]{1,0:T(8,128)}) custom-call(s32[8]{0:T(128)} %sec.3, f32[4,64,512]{2,1,0:T(8,128)} %get-tuple-element.6.states, f32[8,64]{1,0:T(8,128)} %get-tuple-element.7.turned), custom_call_target="tpu_custom_call" | custom-call | tf_op jit(solution)/shard_map/pallas_call | solution.py:641

commit v6 on v5

--- a/solution.py
+++ b/solution.py
@@ -36,13 +36,6 @@
 
 
 def apply_map(x, high, low):
-    rows = x.shape[0]
-    pieces = stacked(x)
-    return folded(dot(pieces, high, ((1,), (1,)))) + dot(pieces[:rows], low, ((1,), (1,)))
-
-
-def product_of(x, y):
-    high, low = halves(y)
     rows = x.shape[0]
     pieces = stacked(x)
     return folded(dot(pieces, high, ((1,), (0,)))) + dot(pieces[:rows], low, ((1,), (0,)))
@@ -97,22 +90,25 @@
             src_ref=src, dst_ref=dst, send_sem=send, recv_sem=recv, device_id=to, device_id_type=MESH
         )
 
-    def section_maps(coupling, order, high_ref, low_ref, own_map):
+    def section_maps(jobs):
         row = lax.broadcasted_iota(jnp.int32, (sub, sub), 0)
         col = lax.broadcasted_iota(jnp.int32, (sub, sub), 1)
-        maps = [jnp.where(row == col, 1.0, 0.0).astype(F32)] * nsub
-        for i, t in enumerate(order):
+        eye = jnp.where(row == col, 1.0, 0.0)
+        maps = [[eye.astype(F32)] * nsub for _ in jobs]
+        for i in range(T):
+            for own, (coupling, order, high_ref, low_ref, _) in zip(maps, jobs):
+                t = order[i]
+                for n in range(nsub):
+                    block = coupling[t, cols(n), :]
+                    if i == 0:
+                        new = -dot(eye.astype(BF16), block, ((1,), (1,)))
+                    else:
+                        new = -couple(own[n], block)
+                    own[n] = select(t, new, own[n])
+                    high_ref[n, :, cols(t)], low_ref[n, :, cols(t)] = halves(own[n])
+        for own, job in zip(maps, jobs):
             for n in range(nsub):
-                block = coupling[t, cols(n), :]
-                if i == 0:
-                    new = -block.astype(F32)
-                else:
-                    both = dot(block, jnp.concatenate(halves(maps[n]), 1), ((1,), (0,)))
-                    new = -(both[:, :sub] + both[:, sub:])
-                maps[n] = select(t, new, maps[n])
-                high_ref[n, cols(t), :], low_ref[n, cols(t), :] = halves(maps[n])
-        for n in range(nsub):
-            own_map[n] = maps[n]
+                job[4][n] = own[n]
 
     def in_order(mine, theirs, lead):
         ahead = jnp.full(mine.shape, core, jnp.int32) == lead
@@ -150,7 +146,7 @@
         for j in range(half):
             one, two = in_order(scan["map"][base + j], scan["mate_map"][j], lead)
             scan["one_h"][j], scan["one_l"][j] = halves(one)
-            both = product_of(two, one)
+            both = apply_map(one, *halves(two))
             scan["chip_map"][j] = both
             scan["chip_h"][j], scan["chip_l"][j] = halves(both)
         pl.when(first_of_pair)(pair_map_copy(scan, way).start)
@@ -226,9 +222,6 @@
         def _():
             pair_map_copy(scan, way).wait_recv()
 
-    def lanes(n):
-        return pl.ds(pl.multiple_of(n * sub, sub), sub)
-
     def scan_end(scan, own, last, first_of_pair, way):
         map_copy(scan).wait_send()
         off_copy(scan, own).wait_send()
@@ -255,9 +248,8 @@
 
     up, down = list(range(T)), list(range(T - 1, -1, -1))
     first_loads[0].wait()
-    section_maps(fc, up, fmap_h, fmap_l, f_scan["map"])
     first_loads[1].wait()
-    section_maps(bc, down, bmap_h, bmap_l, b_scan["map"])
+    section_maps(((fc, up, fmap_h, fmap_l, f_scan["map"]), (bc, down, bmap_h, bmap_l, b_scan["map"])))
     first_loads[2].wait()
     carry = [None] * nsub
     for t in range(T):
@@ -292,15 +284,7 @@
 
     chain(f_scan, f_first, f_last, 0, f_lead, 1)
 
-    def forward_state(t, n):
-        state = driven[t, n] + apply_map(f_scan["into"][n], fmap_h[n, cols(t), :], fmap_l[n, cols(t), :])
-        state = select(t, state, jnp.zeros_like(state))
-        f_split[t, :, lanes(n)] = stacked(state)
-
     if split:
-        for t in down:
-            for j in range(half):
-                forward_state(t, base + j)
         for j in range(half):
             hand_copy(f_scan, j, other_base).wait_recv()
 
@@ -334,8 +318,10 @@
             w_send[q, t, n] += w_pass[t, n]
 
     for t in down:
-        for j in range(half):
-            forward_state(t, other_base + j)
+        for n in range(nsub):
+            state = driven[t, n] + apply_map(f_scan["into"][n], fmap_h[n, :, cols(t)], fmap_l[n, :, cols(t)])
+            state = select(t, state, jnp.zeros_like(state))
+            f_split[t, :, cols(n)] = stacked(state)
 
         if merging:
 
@@ -483,18 +469,13 @@
     join_offsets(b_scan, g_loc.at[0], 1, b_lead, -1)
     chain(b_scan, b_first, b_last, 1, b_lead, -1)
 
-    def backward_states(n):
+    if split:
+        for j in range(half):
+            hand_copy(b_scan, j, other_base).wait_recv()
+    for n in range(nsub):
         states = apply_map(b_scan["into"][n], bmap_h[n], bmap_l[n])
         for t in range(T):
-            sol[t, :, lanes(n)] = g_loc[t, n] + states[:, cols(t)]
-
-    if split:
-        for j in range(half):
-            backward_states(base + j)
-        for j in range(half):
-            hand_copy(b_scan, j, other_base).wait_recv()
-    for j in range(half):
-        backward_states(other_base + j)
+            sol[t, :, cols(n)] = g_loc[t, n] + states[:, cols(t)]
 
     scan_end(f_scan, driven.at[T - 1], f_last, f_lead, 1)
     scan_end(b_scan, g_loc.at[0], b_last, b_lead, -1)
@@ -574,7 +555,7 @@
     nsub = width // sub
     F = arrow_rows.shape[1]
     vmem, hbm = pl.BlockSpec(memory_space=pltpu.VMEM), pl.BlockSpec(memory_space=pl.ANY)
-    maps = pltpu.VMEM((nsub, T * sub, sub), BF16)
+    maps = pltpu.VMEM((nsub, sub, T * sub), BF16)
     dma = pltpu.SemaphoreType.DMA
     others = n_sp - 1
     states, turned = pl.pallas_call(

time: 59.8 us -> 59.1 us (0.988)
  Pallas kernels: 58.7 us -> 58 us
    pallas_call x1, Pallas kernels: 56.8 us -> 56.1 us  [on_device(): pl.pallas_call(functools.partial(kernel, n_tm, n_sp), out_shape=(jax.Shap...]
where the time goes in v6:
time: 59.1 us; the launch traced here: 58.6 us
  Pallas kernels  58 us (98%)
  between operations  0.64 us (1%)
    pallas_call x1, Pallas kernels, on_device(): pl.pallas_call(functools.partial(kernel, n_tm, n_sp), out_shape=(jax.Shap...  56.1 us
    pallas_call x1, Pallas kernels, on_device(): pl.pallas_call(finish, out_shape=(jax.ShapeDtypeStruct(states.shape, F32)...  1.9 us

profile of v6, /device:TPU:0, one launch (start us, length us, event | category | flops | bytes accessed | tf_op | source)
XLA Modules:
  0.0 58.6 jit_solution(17974413693846004628)
XLA Ops:
  0.6 56.1 %shard_map.95 = (f32[4,64,512]{2,1,0:T(8,128)}, f32[8,64]{1,0:T(8,128)}) custom-call(s32[8]{0:T(128)} %sec.3, bf16[4,64,2048]{2,1,0:T(8,128)(2,1)} %rs_hbm.1, f32[8,64]{1,0:T(8,128)} %bitcast.2, bf16[4,512,2048]{2,1,0:T(8,128)(2,1)} %diag_hbm.1, bf16[4,512,128]{2,1,0:T(8,128)(2,1)} %fc_hbm.1, bf16[4,512,128]{2,1,0:T(8,128)(2,1)} %bc_hbm.1, ...), custom_call_target="tpu_custom_call" | custom-call | flops 2147483648 | bytes 8388608 | tf_op jit(solution)/shard_map/pallas_call | solution.py:561
  56.7 1.9 %shard_map.96 = (f32[4,64,512]{2,1,0:T(8,128)}, f32[8,64]{1,0:T(8,128)}) custom-call(s32[8]{0:T(128)} %sec.3, f32[4,64,512]{2,1,0:T(8,128)} %get-tuple-element.6.states, f32[8,64]{1,0:T(8,128)} %get-tuple-element.7.turned), custom_call_target="tpu_custom_call" | custom-call | tf_op jit(solution)/shard_map/pallas_call | solution.py:622

commit v7 on v6

--- a/solution.py
+++ b/solution.py
@@ -42,15 +42,15 @@
 
 
 def kernel(
-    n_tm, n_sp, sec, rs_hbm, tip_side, diag_hbm, fc_hbm, bc_hbm, arrow, tip_inv,
+    n_tm, n_sp, sec, rs, tip_side, diag_hbm, fc, bc, arrow, tip_inv,
     sol, tip_out,
-    rs, fc, bc, diag, fmap_h, fmap_l, bmap_h, bmap_l, driven, f_split, g_loc,
+    diag, fmap_h, fmap_l, bmap_h, bmap_l, driven, f_split, g_loc,
     w_send, w_recv, w_pass, v_send, v_recv, v_own, part, gath_sp, gath_tm, mine_tm,
     f_scan, b_scan,
-    in_sem, diag_sem, ws_sem, wr_sem, ps_sem, pr_sem, vs_sem, vr_sem, as_sem, ar_sem, ts_sem, tr_sem,
+    diag_sem, ws_sem, wr_sem, ps_sem, pr_sem, vs_sem, vr_sem, as_sem, ar_sem, ts_sem, tr_sem,
 ):
-    T, rows = rs_hbm.shape[0], rs_hbm.shape[1]
-    width, sub = fc_hbm.shape[1], fc_hbm.shape[2]
+    T, rows = rs.shape[0], rs.shape[1]
+    width, sub = fc.shape[1], fc.shape[2]
     nsub = width // sub
     F = arrow.shape[1]
     s, p = lax.axis_index("tm"), lax.axis_index("space")
@@ -61,14 +61,10 @@
     other_base = half - core * half if split else 0
     mate = s + 1 - 2 * core
 
-    first_loads = [
-        pltpu.make_async_copy(src, dst, in_sem.at[i])
-        for i, (src, dst) in enumerate(((fc_hbm, fc), (bc_hbm, bc), (rs_hbm, rs)))
-    ]
     loads = [
         pltpu.make_async_copy(diag_hbm.at[t], diag.at[t], diag_sem.at[t]) for t in range(T)
     ]
-    for load in first_loads + loads:
+    for load in loads:
         load.start()
 
     barrier = pltpu.get_barrier_semaphore()
@@ -247,10 +243,7 @@
     f_lead, b_lead = lax.rem(chip, 2) == 0, lax.rem(chip, 2) == 1
 
     up, down = list(range(T)), list(range(T - 1, -1, -1))
-    first_loads[0].wait()
-    first_loads[1].wait()
     section_maps(((fc, up, fmap_h, fmap_l, f_scan["map"]), (bc, down, bmap_h, bmap_l, b_scan["map"])))
-    first_loads[2].wait()
     carry = [None] * nsub
     for t in range(T):
         loads[t].wait()
@@ -566,19 +559,16 @@
         ),
         in_specs=[
             pl.BlockSpec(memory_space=pltpu.SMEM),
+            vmem,
+            vmem,
             hbm,
             vmem,
-            hbm,
-            hbm,
-            hbm,
+            vmem,
             vmem,
             vmem,
         ],
         out_specs=(vmem, vmem),
         scratch_shapes=[
-            pltpu.VMEM(right_side.shape, BF16),
-            pltpu.VMEM(fwd.shape, BF16),
-            pltpu.VMEM(bwd.shape, BF16),
             pltpu.VMEM(diag_inverse.shape, BF16),
             maps,
             maps,
@@ -599,7 +589,6 @@
             pltpu.VMEM((F, 2 * rows), F32),
             scan_scratch(nsub, rows, sub),
             scan_scratch(nsub, rows, sub),
-            dma((3,)),
             dma((T,)),
             dma((others, T, 2)),
             dma((others, T, 2)),

time: 59.1 us -> 58 us (0.981)
  Pallas kernels: 58 us -> 56.9 us
    pallas_call x1, Pallas kernels: 56.1 us -> 55 us  [on_device(): pl.pallas_call(functools.partial(kernel, n_tm, n_sp), out_shape=(jax.Shap...]
where the time goes in v7:
time: 58 us; the launch traced here: 57.5 us
  Pallas kernels  56.9 us (98%)
  between operations  0.64 us (1%)
    pallas_call x1, Pallas kernels, on_device(): pl.pallas_call(functools.partial(kernel, n_tm, n_sp), out_shape=(jax.Shap...  55 us
    pallas_call x1, Pallas kernels, on_device(): pl.pallas_call(finish, out_shape=(jax.ShapeDtypeStruct(states.shape, F32)...  1.9 us

profile of v7, /device:TPU:0, one launch (start us, length us, event | category | flops | bytes accessed | tf_op | source)
XLA Modules:
  0.0 57.5 jit_solution(13423995127539295396)
XLA Ops:
  0.6 55.0 %shard_map.95 = (f32[4,64,512]{2,1,0:T(8,128)}, f32[8,64]{1,0:T(8,128)}) custom-call(s32[8]{0:T(128)} %sec.3, bf16[4,64,2048]{2,1,0:T(8,128)(2,1)} %rs.1, f32[8,64]{1,0:T(8,128)} %bitcast.2, bf16[4,512,2048]{2,1,0:T(8,128)(2,1)} %diag_hbm.1, bf16[4,512,128]{2,1,0:T(8,128)(2,1)} %fc.1, bf16[4,512,128]{2,1,0:T(8,128)(2,1)} %bc.1, bf16[4,8,512]{2,1,0:T(8,128)(2,1)} %arrow.1, ...), custom_call_target="tpu_custom_call" | custom-call | flops 2147483648 | bytes 8388608 | tf_op jit(solution)/shard_map/pallas_call | solution.py:554
  55.6 1.9 %shard_map.96 = (f32[4,64,512]{2,1,0:T(8,128)}, f32[8,64]{1,0:T(8,128)}) custom-call(s32[8]{0:T(128)} %sec.3, f32[4,64,512]{2,1,0:T(8,128)} %get-tuple-element.6.states, f32[8,64]{1,0:T(8,128)} %get-tuple-element.7.turned), custom_call_target="tpu_custom_call" | custom-call | tf_op jit(solution)/shard_map/pallas_call | solution.py:611

commit v8 on v7

--- a/solution.py
+++ b/solution.py
@@ -138,14 +138,14 @@
     def away(way, steps):
         return lax.rem(s + n_tm + way * steps, n_tm)
 
-    def join_maps(scan, lead, first_of_pair, way):
+    def join_maps(scan, lead, first, first_of_pair, way):
         for j in range(half):
             one, two = in_order(scan["map"][base + j], scan["mate_map"][j], lead)
             scan["one_h"][j], scan["one_l"][j] = halves(one)
             both = apply_map(one, *halves(two))
             scan["chip_map"][j] = both
             scan["chip_h"][j], scan["chip_l"][j] = halves(both)
-        pl.when(first_of_pair)(pair_map_copy(scan, way).start)
+        pl.when(jnp.logical_and(first_of_pair, jnp.logical_not(first)))(pair_map_copy(scan, way).start)
 
     def join_offsets(scan, own, lead, first_of_pair, way):
         off_copy(scan, own).wait_recv()
@@ -214,17 +214,14 @@
                 hand_copy(scan, j, base).start()
             scan["into"][base + j] = mine
 
-        @pl.when(jnp.logical_and(second, first))
-        def _():
-            pair_map_copy(scan, way).wait_recv()
-
-    def scan_end(scan, own, last, first_of_pair, way):
+    def scan_end(scan, own, first, last, first_of_pair, way):
         map_copy(scan).wait_send()
         off_copy(scan, own).wait_send()
 
+        pl.when(jnp.logical_and(first_of_pair, jnp.logical_not(first)))(pair_map_copy(scan, way).wait_send)
+
         @pl.when(first_of_pair)
         def _():
-            pair_map_copy(scan, way).wait_send()
             for j in range(half):
                 pair_off_copy(scan, j, way).wait_send()
 
@@ -258,9 +255,6 @@
     map_copy(f_scan).start()
     off_copy(f_scan, driven.at[T - 1]).start()
     map_copy(b_scan).start()
-    map_copy(f_scan).wait_recv()
-    join_offsets(f_scan, driven.at[T - 1], 0, f_lead, 1)
-    join_maps(f_scan, 0, f_lead, 1)
 
     def early():
         for q in range(n_sp - 1):
@@ -274,6 +268,10 @@
                 remote(v_send.at[q], v_recv.at[p - 1], vs_sem.at[q], vr_sem.at[p - 1], {"space": q}).start()
 
     pl.when(chip >= chips // 2)(early)
+
+    map_copy(f_scan).wait_recv()
+    join_offsets(f_scan, driven.at[T - 1], 0, f_lead, 1)
+    join_maps(f_scan, 0, f_first, f_lead, 1)
 
     chain(f_scan, f_first, f_last, 0, f_lead, 1)
 
@@ -377,7 +375,7 @@
 
     pl.when(chip < chips // 2)(early)
     map_copy(b_scan).wait_recv()
-    join_maps(b_scan, 1, b_lead, -1)
+    join_maps(b_scan, 1, b_first, b_lead, -1)
 
     own_cols = pl.ds(pl.multiple_of(p * width, width), width)
     for t in range(T):
@@ -470,8 +468,8 @@
         for t in range(T):
             sol[t, :, cols(n)] = g_loc[t, n] + states[:, cols(t)]
 
-    scan_end(f_scan, driven.at[T - 1], f_last, f_lead, 1)
-    scan_end(b_scan, g_loc.at[0], b_last, b_lead, -1)
+    scan_end(f_scan, driven.at[T - 1], f_first, f_last, f_lead, 1)
+    scan_end(b_scan, g_loc.at[0], b_first, b_last, b_lead, -1)
     for q in range(n_sp - 1):
 
         @pl.when(p > q)

time: 58 us -> 57.9 us (level)
  no operation moved by 1% of the time
where the time goes in v8:
time: 57.9 us; the launch traced here: 57.4 us
  Pallas kernels  56.8 us (98%)
  between operations  0.64 us (1%)
    pallas_call x1, Pallas kernels, on_device(): pl.pallas_call(functools.partial(kernel, n_tm, n_sp), out_shape=(jax.Shap...  54.9 us
    pallas_call x1, Pallas kernels, on_device(): pl.pallas_call(finish, out_shape=(jax.ShapeDtypeStruct(states.shape, F32)...  1.9 us

profile of v8, /device:TPU:0, one launch (start us, length us, event | category | flops | bytes accessed | tf_op | source)
XLA Modules:
  0.0 57.4 jit_solution(13042398671260272765)
XLA Ops:
  0.6 54.9 %shard_map.95 = (f32[4,64,512]{2,1,0:T(8,128)}, f32[8,64]{1,0:T(8,128)}) custom-call(s32[8]{0:T(128)} %sec.3, bf16[4,64,2048]{2,1,0:T(8,128)(2,1)} %rs.1, f32[8,64]{1,0:T(8,128)} %bitcast.2, bf16[4,512,2048]{2,1,0:T(8,128)(2,1)} %diag_hbm.1, bf16[4,512,128]{2,1,0:T(8,128)(2,1)} %fc.1, bf16[4,512,128]{2,1,0:T(8,128)(2,1)} %bc.1, bf16[4,8,512]{2,1,0:T(8,128)(2,1)} %arrow.1, ...), custom_call_target="tpu_custom_call" | custom-call | flops 2147483648 | bytes 8388608 | tf_op jit(solution)/shard_map/pallas_call | solution.py:552
  55.5 1.9 %shard_map.96 = (f32[4,64,512]{2,1,0:T(8,128)}, f32[8,64]{1,0:T(8,128)}) custom-call(s32[8]{0:T(128)} %sec.3, f32[4,64,512]{2,1,0:T(8,128)} %get-tuple-element.6.states, f32[8,64]{1,0:T(8,128)} %get-tuple-element.7.turned), custom_call_target="tpu_custom_call" | custom-call | tf_op jit(solution)/shard_map/pallas_call | solution.py:609
